TPU v7x, 256 devices: a whole 4x4x8 slice. The times are simulated.
256 devices in a mesh: wide: 32 (over y, z_hi, core), narrow: 8 (over z_lo, x).
Axes of the slice: x: 4, y: 4, z: 8 (z_hi: 4, z_lo: 2; z = z_hi * 2 + z_lo), core: 2. Of those that a mesh axis runs over, the one named last changes fastest.
Arguments:
- images: bfloat16 [24576, 512], P('wide'), may hold values from -20 to 20
- captions: bfloat16 [24576, 512], P(('wide', 'narrow')), may hold values from -20 to 20
- taxon_paths: int32 [7, 24576], P(None, 'wide'), may hold values from 0 to 2047, as said below
- sample_weight: float32 [24576], P('wide'), may hold values from 2 to 20
- depth_weight: float32 [8], replicated, may hold values from 0.1 to 10
Outputs:
- grad_images: float32 [24576, 512], P(('wide', 'narrow'))
- grad_captions: float32 [24576, 512], P(('wide', 'narrow'))
Inputs may be any that keep to these rules, and one draw needn't show every extreme that they name: `taxon_paths`: A taxon id at one rank determines the ids at all ranks before it.
All inputs are finite; a program needn't handle non-finite values.
Results may differ from a plain program's by a relative error of at most 0.0039.
Values may be sent and summed in bfloat16 or wider, within the bound.
A program may use at most 128 MiB of HBM per device.

v0:
```python
import jax
import jax.numpy as jnp
from jax import lax
from jax.sharding import PartitionSpec as P


def caption_weights(image_paths, caption_paths, depth_weight):
    matched = jnp.ones((image_paths.shape[1], caption_paths.shape[0]), jnp.bool_)
    depth_count = jnp.zeros(matched.shape, jnp.int32)
    for rank_level in range(image_paths.shape[0]):
        same_id = image_paths[rank_level][:, None] == caption_paths[:, rank_level][None, :]
        matched = jnp.logical_and(matched, same_id)
        depth_count = depth_count + matched.astype(jnp.int32)
    weights = jnp.zeros(depth_count.shape, jnp.float32)
    for depth_level in range(depth_weight.shape[0]):
        weights = weights + jnp.where(depth_count == depth_level, depth_weight[depth_level], 0.0)
    return weights


def body(images, captions, taxon_paths, sample_weight, depth_weight):
    row_count, embed_width = images.shape
    score_scale = embed_width ** (-0.5)
    cap_count = captions.shape[0]
    own_paths = lax.dynamic_slice_in_dim(
        taxon_paths, lax.axis_index("narrow") * cap_count, cap_count, 1
    ).T
    caption_piece = lax.all_gather(captions, "wide", axis=0, tiled=True)
    row_peak = jnp.full((row_count,), -jnp.inf, jnp.float32)
    exp_total = jnp.zeros((row_count,), jnp.float32)
    moments = jnp.zeros((2 * row_count, embed_width), jnp.float32)
    scores = score_scale * jnp.dot(images, caption_piece.T, preferred_element_type=jnp.float32)
    weights = caption_weights(
        taxon_paths, lax.all_gather(own_paths, "wide", axis=0, tiled=True), depth_weight
    )
    new_peak = jnp.max(scores, axis=1)
    shrink = jnp.exp(row_peak - new_peak)
    exp_scores = jnp.exp(scores - new_peak[:, None])
    stacked = jnp.concatenate(
        [exp_scores.astype(jnp.bfloat16), weights.astype(jnp.bfloat16)], axis=0
    )
    product = jnp.dot(stacked, caption_piece, preferred_element_type=jnp.float32)
    rescale = jnp.concatenate([shrink, jnp.ones_like(shrink)])
    moments = moments * rescale[:, None] + product
    row_peak, exp_total, weight_total, moments = (
        new_peak,
        exp_total * shrink + jnp.sum(exp_scores, axis=1),
        jnp.sum(weights, axis=1),
        moments,
    )
    all_caps, all_paths = (
        lax.all_gather(captions, "wide", axis=0, tiled=True),
        lax.all_gather(own_paths, "wide", axis=0, tiled=True),
    )
    global_peak = lax.pmax(row_peak, "narrow")
    global_exp, global_weight = lax.psum(
        (exp_total * jnp.exp(row_peak - global_peak), weight_total), "narrow"
    )
    row_factor = score_scale * sample_weight[:, None]
    own_ratio = jnp.exp(row_peak - global_peak) / global_exp
    local_part = row_factor * (
        moments[:row_count] * own_ratio[:, None] - moments[row_count:] / global_weight[:, None]
    )
    grad_images = lax.psum_scatter(local_part, "narrow", scatter_dimension=0, tiled=True)
    scores = score_scale * jnp.dot(images, all_caps.T, preferred_element_type=jnp.float32)
    weights = caption_weights(taxon_paths, all_paths, depth_weight)
    probability = jnp.exp(scores - global_peak[:, None]) / global_exp[:, None]
    grad_scores = (
        sample_weight[:, None] * (probability - weights / global_weight[:, None])
    ).astype(jnp.bfloat16)
    grad_captions = lax.psum_scatter(
        score_scale * jnp.dot(grad_scores.T, images, preferred_element_type=jnp.float32),
        "wide",
        scatter_dimension=0,
        tiled=True,
    )
    return (grad_images, grad_captions)


def solution(mesh):
    return jax.shard_map(
        body,
        mesh=mesh,
        in_specs=(P("wide", None), P(("wide", "narrow"), None), P(None, "wide"), P("wide"), P()),
        out_specs=(P(("wide", "narrow"), None), P(("wide", "narrow"), None)),
        check_vma=False,
    )
```

profile of v0, /device:TPU:1, one launch (start us, length us, event | category | flops | bytes accessed | tf_op | source)
XLA Modules:
  0.0 321.8 jit_solution(16864725068060496894)
XLA Ops:
  7.2 0.0 copy-start
  7.2 0.0 all-gather.3.cloned.1.call-start
  7.2 0.7 all-gather.3.cloned.1.call-update
  7.9 0.0 reduce-scatter.3.cloned.1.call-start
  8.0 1.1 slice_reduce_fusion.6
  9.0 0.8 dynamic-slice_bitcast_fusion
  9.8 49.4 %all-gather = s32[32,96,7]{1,2,0:T(8,128)S(1)} all-gather(s32[1,96,7]{1,2,0:T(8,128)S(1)} %dynamic-slice_bitcast_fusion), channel_id=1, replica_groups=mesh['wide'=32,'narrow'=8] {'wide'}, dimensions={0}, use_global_device_ids=true | all-gather | bytes 88704 | tf_op jit(solution)/shard_map/all_gather | solution.py:33
  59.3 0.1 reshape.28
  59.4 0.1 fusion.31
  59.5 0.7 broadcast_multiply_fusion
  60.2 1.6 fusion.32
  61.8 22.2 %fusion.16 = bf16[768,3072]{1,0:T(8,128)(2,1)} fusion(f32[]{:T(128)} %bitcast.16, f32[]{:T(128)} %bitcast.15, f32[]{:T(128)} %bitcast.14, f32[]{:T(128)} %bitcast.13, f32[]{:T(128)} %bitcast.12, f32[]{:T(128)} %bitcast.11, f32[]{:T(128)} %bitcast.10, f32[]{:T(128)} %bitcast.9, s32[3072]{0:T(1024)S(1)} %bitcast.28, s32[768]{0:T(1024)S(1)} %get-tuple-element.7, ...), kind=kLoop, calls=%fused_computation.21 | loop fusion | flops 117964800 | bytes 4826144 | tf_op jit(solution)/shard_map/convert_element_type | solution.py:39
  84.0 21.2 %fusion.15 = f32[768]{0:T(1024)S(1)} fusion(f32[]{:T(128)} %bitcast.16, f32[]{:T(128)} %bitcast.15, f32[]{:T(128)} %bitcast.14, f32[]{:T(128)} %bitcast.13, f32[]{:T(128)} %bitcast.12, f32[]{:T(128)} %bitcast.11, f32[]{:T(128)} %bitcast.10, f32[]{:T(128)} %bitcast.9, s32[3072]{0:T(1024)S(1)} %bitcast.29, s32[768]{0:T(1024)S(1)} %get-tuple-element.7, ...), kind=kLoop, calls=%fused_computation.20 | loop fusion | flops 117964032 | bytes 110624 | tf_op jit(solution)/shard_map/reduce_sum | solution.py:47
  105.2 0.0 all-gather.3.cloned.1.call-done
  105.3 0.0 copy-done
  105.3 7.0 %multiply_reduce_fusion = (f32[768]{0:T(1024)S(1)}, f32[768,3072]{1,0:T(8,128)}) fusion(bf16[768,512]{1,0:T(8,128)(2,1)S(1)} %copy-done, bf16[3072,512]{1,0:T(8,128)(2,1)} %all-gather.3.cloned.1.call-done), kind=kOutput, calls=%fused_computation.17 | convolution fusion | flops 2420636928 | bytes 13372416 | tf_op jit(solution)/shard_map/dot_general | solution.py:31
  112.3 15.1 %pmax.7 = f32[768]{0:T(1024)S(1)} all-reduce(f32[768]{0:T(1024)S(1)} %get-tuple-element.30), channel_id=1, replica_groups=mesh['wide'=32,'narrow'=8] {'narrow'}, use_global_device_ids=true, to_apply=%region_1.2 | all-reduce | flops 768 | bytes 6144 | tf_op jit(solution)/shard_map/pmax | solution.py:54
  127.4 7.6 %fusion.10 = (f32[768]{0:T(1024)S(1)}, bf16[768,3072]{1,0:T(8,128)(2,1)}) fusion(f32[768,3072]{1,0:T(8,128)} %get-tuple-element.31, f32[768]{0:T(1024)S(1)} %get-tuple-element.30), kind=kLoop, calls=%fused_computation.15 | loop fusion | flops 9436416 | bytes 14161920 | tf_op jit(solution)/shard_map/reduce_sum | solution.py:46
  135.0 12.9 %all-reduce.1 = (f32[768]{0:T(1024)S(1)}, f32[768]{0:T(1024)S(1)}) all-reduce(f32[768]{0:T(1024)S(1)} %fusion.15, f32[768]{0:T(1024)S(1)} %add_multiply_fusion), channel_id=1, replica_groups=mesh['wide'=32,'narrow'=8] {'narrow'}, use_global_device_ids=true, to_apply=%region_5.6 | all-reduce | flops 1536 | bytes 12288 | tf_op jit(solution)/shard_map/psum | solution.py:55
  147.9 0.0 copy-start.1
  147.9 8.8 %fusion.12 = f32[1536,512]{1,0:T(8,128)S(1)} fusion(bf16[3072,512]{1,0:T(8,128)(2,1)} %all-gather.3.cloned.1.call-done, bf16[768,3072]{1,0:T(8,128)(2,1)} %fusion.16, bf16[768,3072]{1,0:T(8,128)(2,1)} %get-tuple-element.12, f32[1536]{0:T(1024)S(1)} %pad_multiply_fusion), kind=kOutput, calls=%fused_computation.19 | convolution fusion | flops 4851499008 | bytes 15734784 | tf_op jit(solution)/shard_map/dot_general | solution.py:41
  156.7 1.5 fusion.18
  158.3 0.0 reduce-scatter.3.cloned.1.call-update
  158.3 0.0 reduce-scatter.5.cloned.1.call-start
  158.3 0.0 copy-done.1
  158.3 30.6 %convolution_multiply_fusion = f32[3072,512]{1,0:T(8,128)} fusion(bf16[768,512]{1,0:T(8,128)(2,1)S(1)} %copy-done, f32[768,3072]{1,0:T(8,128)} %get-tuple-element.31, f32[768]{0:T(1024)S(1)} %get-tuple-element.9, f32[768]{0:T(1024)S(1)} %get-tuple-element.10, f32[768]{0:T(1024)S(1)} %pmax.7, f32[768]{0:T(1024)S(1)} %copy-done.1, f32[]{:T(128)} %bitcast.16, ...), kind=kOutput, calls=%fused_computation.18 | convolution fusion | flops 2549612544 | bytes 16634912 | tf_op jit(solution)/shard_map/dot_general | solution.py:71
  188.9 0.0 reduce-scatter.5.cloned.1.call-update
  188.9 9.1 %reduce-scatter.3.cloned.1.call-done = f32[96,512]{1,0:T(8,128)} async-done(((f32[768,512]{1,0:T(8,128)}), f32[96,512]{1,0:T(8,128)}) %reduce-scatter.3.cloned.1.call-update) | async-done | bytes 196624 | tf_op jit(solution)/shard_map/reduce_scatter | solution.py:63
  198.1 117.2 %reduce-scatter.5.cloned.1.call-done = f32[96,512]{1,0:T(8,128)} async-done(((f32[3072,512]{1,0:T(8,128)}), f32[96,512]{1,0:T(8,128)}) %reduce-scatter.5.cloned.1.call-update) | async-done | bytes 196624 | tf_op jit(solution)/shard_map/reduce_scatter | solution.py:70
  (4 shorter events, 0.0 us)
Async XLA Ops:
  7.2 98.1 %copy-start = (bf16[768,512]{1,0:T(8,128)(2,1)S(1)}, bf16[768,512]{1,0:T(8,128)(2,1)}, u32[]{:S(2)}) copy-start(bf16[768,512]{1,0:T(8,128)(2,1)} %param.5) | copy-start | bytes 2359300
  7.2 98.1 %all-gather.3.cloned.1.call-start = ((), (), s32[]{:S(2)}) async-start(), calls=%async_computation.2 | async-start | bytes 3244032 | tf_op jit(solution)/shard_map/all_gather | solution.py:27
  7.9 190.2 %reduce-scatter.3.cloned.1.call-start = ((), (), s32[]{:S(2)}) async-start(), calls=%async_computation.3 | async-start | bytes 1769472 | tf_op jit(solution)/shard_map/reduce_scatter | solution.py:63
  147.9 10.4 %copy-start.1 = (f32[768]{0:T(1024)S(1)}, f32[768]{0:T(1024)}, u32[]{:S(2)}) copy-start(f32[768]{0:T(1024)} %param.8) | copy-start | bytes 9220
  158.3 157.0 %reduce-scatter.5.cloned.1.call-start = ((), (), s32[]{:S(2)}) async-start(), calls=%async_computation.4 | async-start | bytes 6488064 | tf_op jit(solution)/shard_map/reduce_scatter | solution.py:70
Sparse Core Ops, SparseCore 0:
  10.6 61.4 all-gather.2
  158.4 39.6 reduce-scatter.2
  202.7 112.5 reduce-scatter.4
where the time goes:
time: 323 us; the launch traced here: 322 us
  waiting for transfers between devices  127 us (39%)
  blocking collectives  77.5 us (24%)
  other arithmetic  53.3 us (17%)
  matrix products  46.4 us (14%)
  between operations  13.8 us (4%)
  local copies, waits for them, and re-layouts  3.68 us (1%)
    reduce_scatter x1, waiting for transfers between devices, body(): lax.psum_scatter(score_scale * jnp.dot(grad_scores.T, images, preferred_e...  117 us
    all_gather x1, blocking collectives, body(): lax.all_gather(own_paths, 'wide', axis=0, tiled=True)  49.4 us
    dot_general x1, matrix products, body(): jnp.dot(grad_scores.T, images, preferred_element_type=jnp.float32)  30.6 us
    convert_element_type x1, other arithmetic, body(): weights.astype(jnp.bfloat16)  22.2 us
    reduce_sum x1, other arithmetic, body(): jnp.sum(weights, axis=1)  21.2 us
    pmax x1, blocking collectives, body(): global_peak = lax.pmax(row_peak, 'narrow')  15.1 us
    psum x1, blocking collectives, body(): lax.psum((exp_total * jnp.exp(row_peak - global_peak), weight_total), 'na...  12.9 us
    reduce_scatter x1, waiting for transfers between devices, body(): lax.psum_scatter(local_part, 'narrow', scatter_dimension=0, tiled=True)  9.11 us
  transfers between devices with their start and end apart: 3, of which 2 were waited for; matrix products, arithmetic and copies ran while one was open for 24% of the time, Pallas kernels for 0%

commit v1 on v0

v1 whole, which is shorter than its diff:
```python
import functools
import math

import jax
import jax.numpy as jnp
from jax import lax
from jax.experimental import pallas as pl
from jax.experimental.pallas import tpu as pltpu
from jax.sharding import PartitionSpec as P

BF16, F32 = jnp.bfloat16, jnp.float32
NY, NH, NX, NL = 4, 4, 4, 2
ARRIVE = (0, 3, 1, 2)
LEAVE = (2, 1, 3, 0)


def kernel(
    img_ref, cap_ref, tax_ref, sw_ref, dw_ref, gi_ref, gc_ref,
    caps, img_t, ids, e_buf, t_buf, e_low, t_low, acc_e, acc_t, peaks, stat_out, stat_in,
    p_own, p_out, p_in, a_out, a_in, b_out, b_in, za_out, za_in, zb_out, zb_in,
    x_out, x_in, l_out, l_in,
    cap_send, cap_recv, id_send, id_recv, stat_send, stat_recv,
    p_send, p_recv, a_send, a_recv, b_send, b_recv, za_send, za_recv, zb_send, zb_recv,
    x_send, x_recv, l_send, l_recv,
):
    rows, width = img_ref.shape
    own = cap_ref.shape[0]
    half = own // 2
    pair = 2 * own
    ranks = tax_ref.shape[0]
    scale = width ** -0.5
    to_exp2 = scale * math.log2(math.e)

    wide, narrow = lax.axis_index("wide"), lax.axis_index("narrow")
    core, h, y = wide % 2, (wide // 2) % NH, wide // (2 * NH)
    x, low = narrow % NX, narrow // NX

    def chip(dy, dh):
        return ((y + dy) % NY) * NH + (h + dh) % NH

    def slot(dy, dh, dc=0):
        return chip(dy, dh) * 2 + (core + dc) % 2

    def at_wide(dy, dh, dc=0):
        return {"wide": slot(dy, dh, dc)}

    def at_narrow(dx, dl):
        return {"narrow": ((low + dl) % NL) * NX + (x + dx) % NX}

    barrier = pltpu.get_barrier_semaphore()
    partners = [at_wide(0, 0, 1)]
    partners += [at_wide(0, d) for d in range(1, NH)] + [at_wide(d, 0) for d in range(1, NY)]
    partners += [at_narrow(dx, dl) for dl in range(NL) for dx in range(NX) if dx or dl]
    for partner in partners:
        pl.semaphore_signal(barrier, inc=1, device_id=partner, device_id_type=pl.DeviceIdType.MESH)

    sent = []

    def send(src, dst, send_sem, recv_sem, where):
        copy = pltpu.make_async_remote_copy(
            src_ref=src, dst_ref=dst, send_sem=send_sem, recv_sem=recv_sem,
            device_id=where, device_id_type=pl.DeviceIdType.MESH,
        )
        copy.start()
        sent.append(copy)

    def arrived(dst, recv_sem):
        pltpu.make_async_copy(dst, dst, recv_sem).wait()

    caps[pl.ds(wide, 1)] = cap_ref[...][None]
    all_ids = jnp.concatenate([tax_ref[...], jnp.zeros((8 - ranks, rows), jnp.int32)], axis=0)
    own_ids = pltpu.roll(all_ids, (rows - own * narrow) % rows, 1)[:, :128]
    ids[pl.ds(wide, 1)] = own_ids[None]

    pl.semaphore_wait(barrier, len(partners))

    cap_sends = iter(range(64))

    def send_caps(s, where, begin=0, size=own):
        k = next(cap_sends)
        piece = caps.at[s, pl.ds(begin, size)]
        send(piece, piece, cap_send.at[k], cap_recv.at[s], where)

    def caps_arrived(s):
        arrived(caps.at[s], cap_recv.at[s])

    mine = ids.at[pl.ds(wide, 1)]
    send(mine, mine, id_send.at[0], id_recv.at[0], at_wide(0, 0, 1))
    send_caps(wide, at_wide(1, 0))
    send_caps(wide, at_wide(3, 0))
    send_caps(wide, at_wide(0, 1))
    send_caps(wide, at_wide(0, 3))
    send_caps(wide, at_wide(0, 0, 1))
    other = ids.at[pl.ds(slot(0, 0, 1), 1)]
    arrived(other, id_recv.at[0])
    both = ids.at[pl.ds(2 * chip(0, 0), 2)]
    for d in range(1, NH):
        send(both, both, id_send.at[d], id_recv.at[NH - d], at_wide(0, d))

    img_t[...] = img_ref[...].T
    peaks[...] = jnp.full_like(peaks, -jnp.inf)

    for d in range(1, NH):
        theirs = ids.at[pl.ds(2 * chip(0, d), 2)]
        arrived(theirs, id_recv.at[d])
    column = ids.at[pl.ds(2 * NH * y, 2 * NH)]
    for d in range(1, NY):
        send(column, column, id_send.at[NH - 1 + d], id_recv.at[NH - 1 + NY - d], at_wide(d, 0))

    def targets(dh, first, count, total):
        def step(i, total):
            dy, c = first + i // 2, i % 2
            g = chip(dy, dh)
            turned = ids[2 * g + c].T
            for r in range(0, own, 32):
                weight = jnp.full((32, rows), dw_ref[0], F32)
                for k in range(ranks):
                    same = turned[r : r + 32, k : k + 1] == tax_ref[k : k + 1, :]
                    weight = jnp.where(same, dw_ref[k + 1], weight)
                t_buf[g, pl.ds(c * own + r, 32), :] = weight
                t_low[dh, dy, pl.ds(c * own + r, 32), :] = weight.astype(BF16)
                total = total + jnp.sum(weight.reshape(4, 8, rows), axis=0)
            return total

        return lax.fori_loop(0, 2 * count, step, total)

    def scores(dh, order, peak, total):
        def product(dy, biggest):
            g = chip(dy, dh)
            block = caps[pl.ds(2 * g, 2)].reshape(pair, width)
            s = jnp.dot(block, img_t[...], preferred_element_type=F32)
            e_buf[g] = s
            return jnp.maximum(biggest, jnp.max(s.reshape(pair // 8, 8, rows), axis=0))

        biggest = lax.fori_loop(0, NY, product, jnp.broadcast_to(peak, (8, rows)))
        new_peak = jnp.max(biggest, axis=0, keepdims=True)
        shrink = jnp.exp2((peak - new_peak) * to_exp2)

        def exponentials(dy, part):
            g = chip(dy, dh)
            e = jnp.exp2((e_buf[g] - new_peak) * to_exp2)
            e_buf[g] = e
            e_low[dy] = e.astype(BF16)
            return part + jnp.sum(e.reshape(pair // 8, 8, rows), axis=0)

        part = lax.fori_loop(0, NY, exponentials, jnp.zeros((8, rows), F32))
        peaks[pl.ds(order, 1)] = new_peak
        return new_peak, shrink, total * shrink + jnp.sum(part, axis=0, keepdims=True)

    def moments(dh, shrink, first):
        block = jnp.concatenate(
            [caps[pl.ds(2 * chip(dy, dh), 2)].reshape(pair, width) for dy in range(NY)], axis=0
        )
        turned = block.T
        for j in range(0, rows, 256):
            cut = slice(j, j + 256)
            new_e = jnp.dot(turned, e_low[:, :, cut].reshape(NY * pair, 256), preferred_element_type=F32)
            new_t = jnp.dot(turned, t_low[dh, :, :, cut].reshape(NY * pair, 256), preferred_element_type=F32)
            if first:
                acc_e[:, cut] = new_e
                acc_t[:, cut] = new_t
            else:
                acc_e[:, cut] = acc_e[:, cut] * shrink[:, cut] + new_e
                acc_t[:, cut] = acc_t[:, cut] + new_t

    def column_in(dh):
        s = slot(0, dh)
        caps_arrived(s)
        send_caps(s, at_wide(1, 0))
        send_caps(s, at_wide(3, 0))
        if dh == 3:
            send_caps(s, at_wide(0, 1), 0, half)
        if dh == 1:
            send_caps(s, at_wide(0, 3), half, half)
        send_caps(s, at_wide(0, 0, 1))

    def sides_in(dh):
        for dy, on, begin in ((3, 1, 0), (1, 3, half)):
            s = slot(dy, dh)
            caps_arrived(s)
            send_caps(s, at_wide(on, 0), begin, half)
            send_caps(s, at_wide(0, 0, 1))

    def far_in(dh):
        s = slot(2, dh)
        caps_arrived(s)
        send_caps(s, at_wide(0, 0, 1))

    def others_in(dh):
        for dy in range(NY):
            caps_arrived(slot(dy, dh, 1))

    peak = jnp.full((1, rows), -jnp.inf, F32)
    exp_total = jnp.zeros((1, rows), F32)
    t_total = jnp.zeros((8, rows), F32)

    for order, dh in enumerate(ARRIVE):
        if order == 0:
            t_total = targets(dh, 0, 1, t_total)
        sides_in(dh)
        if order == 0:
            column_in(3)
            column_in(1)
            for d in range(1, NY):
                theirs = ids.at[pl.ds(2 * NH * ((y + d) % NY), 2 * NH)]
                arrived(theirs, id_recv.at[NH - 1 + d])
            t_total = targets(dh, 1, NY - 1, t_total)
        if order == 1:
            column_in(2)
        far_in(dh)
        others_in(dh)
        peak, shrink, exp_total = scores(dh, order, peak, exp_total)
        if order < NH - 1:
            t_total = targets(ARRIVE[order + 1], 0, NY, t_total)
            moments(dh, shrink, order == 0)

    stat_out[...] = jnp.concatenate(
        [peak, exp_total, jnp.sum(t_total, axis=0, keepdims=True), jnp.zeros((5, rows), F32)], axis=0
    )
    k = 0
    for dl in range(NL):
        for dx in range(NX):
            if dx or dl:
                back = ((NL - dl) % NL) * NX + (NX - dx) % NX
                send(stat_out, stat_in.at[back], stat_send.at[k], stat_recv.at[back], at_narrow(dx, dl))
                k += 1
    moments(ARRIVE[-1], shrink, False)
    for k in range(1, NL * NX):
        arrived(stat_in.at[k], stat_recv.at[k])
    stats = [stat_out[...]] + [stat_in[k] for k in range(1, NL * NX)]
    top = functools.reduce(jnp.maximum, [s[0:1] for s in stats])
    exp_all = sum(s[1:2] * jnp.exp2((s[0:1] - top) * to_exp2) for s in stats)
    t_all = sum(s[2:3] for s in stats)
    factor_e = sw_ref[...] / exp_all
    factor_t = sw_ref[...] / t_all

    def terms(dy, dh):
        g, k = chip(dy, dh), dy * NH + dh
        to_e = factor_e * jnp.exp2((peaks[ARRIVE.index(dh) : ARRIVE.index(dh) + 1] - top) * to_exp2)
        grad = (to_e * e_buf[g] - factor_t * t_buf[g]).astype(BF16)
        p_own[k] = scale * jnp.dot(grad, img_ref[...], preferred_element_type=F32)
        p_out[k] = p_own[k, pl.ds((1 - core) * own, own), :].astype(BF16)
        send(p_out.at[k], p_in.at[k], p_send.at[k], p_recv.at[k], at_wide(0, 0, 1))

    def chip_sum(dy, dh):
        k = dy * NH + dh
        arrived(p_in.at[k], p_recv.at[k])
        return p_own[k, pl.ds(core * own, own), :] + p_in[k].astype(F32)

    def finish(dy, dh):
        value = chip_sum(dy, dh)
        if dy == 2:
            a_out[dh] = value.astype(BF16)
            for side, (begin, on) in enumerate(((0, 1), (half, 3))):
                cut = pl.ds(begin, half)
                send(a_out.at[dh, cut], a_in.at[dh, cut], a_send.at[dh, side], a_recv.at[dh, side], at_wide(on, 0))
        elif dy in (1, 3):
            side = 0 if dy == 1 else 1
            cut = pl.ds(side * half, half)
            arrived(a_in.at[dh, cut], a_recv.at[dh, side])
            gained = a_in[dh, side * half : (side + 1) * half].astype(F32)
            parts = [value[:half], value[half:]]
            parts[side] = parts[side] + gained
            b_out[dh, side] = jnp.concatenate(parts, axis=0).astype(BF16)
            send(b_out.at[dh, side], b_in.at[dh, side], b_send.at[dh, side], b_recv.at[dh, side], at_wide(dy, 0))
        else:
            for side in (0, 1):
                arrived(b_in.at[dh, side], b_recv.at[dh, side])
                value = value + b_in[dh, side].astype(F32)
            if dh == 2:
                za_out[...] = value.astype(BF16)
                for side, (begin, on) in enumerate(((0, 1), (half, 3))):
                    cut = pl.ds(begin, half)
                    send(za_out.at[cut], za_in.at[cut], za_send.at[side], za_recv.at[side], at_wide(0, on))
            elif dh in (1, 3):
                side = 0 if dh == 1 else 1
                arrived(za_in.at[pl.ds(side * half, half)], za_recv.at[side])
                gained = za_in[side * half : (side + 1) * half].astype(F32)
                parts = [value[:half], value[half:]]
                parts[side] = parts[side] + gained
                zb_out[side] = jnp.concatenate(parts, axis=0).astype(BF16)
                send(zb_out.at[side], zb_in.at[side], zb_send.at[side], zb_recv.at[side], at_wide(0, dh))
            else:
                for side in (0, 1):
                    arrived(zb_in.at[side], zb_recv.at[side])
                    value = value + zb_in[side].astype(F32)
                gc_ref[...] = value

    def image_terms():
        own_e = scale * factor_e * jnp.exp2((peak - top) * to_exp2)
        own_t = scale * factor_t
        turned = (acc_e[...] * own_e - acc_t[...] * own_t).T
        x_out[...] = turned.reshape(NL, NX, own, width).astype(BF16)
        for d in range(1, NX):
            to = (x + d) % NX
            send(x_out.at[:, to], x_in.at[NX - d], x_send.at[d], x_recv.at[NX - d], at_narrow(d, 0))

    def image_sum():
        for d in range(1, NX):
            arrived(x_in.at[d], x_recv.at[d])

        def total(which):
            value = x_out[which, x].astype(F32)
            for d in range(1, NX):
                value = value + x_in[d, which].astype(F32)
            return value

        l_out[...] = total(1 - low).astype(BF16)
        send(l_out, l_in, l_send.at[0], l_recv.at[0], at_narrow(0, 1))
        gi_ref[...] = total(low)

    def image_finish():
        arrived(l_in, l_recv.at[0])
        gi_ref[...] = gi_ref[...] + l_in[...].astype(F32)

    steps = [(2, dh) for dh in LEAVE]
    for dh in LEAVE:
        steps += [(1, dh), (3, dh)]
    steps += [(0, dh) for dh in LEAVE]
    lag = 2
    for i, step in enumerate(steps):
        terms(*step)
        if i == 4:
            image_terms()
        if i >= lag:
            finish(*steps[i - lag])
        if i == 13:
            image_sum()
    for step in steps[len(steps) - lag :]:
        finish(*step)
    image_finish()
    for copy in sent:
        copy.wait_send()


def body(images, captions, taxon_paths, sample_weight, depth_weight):
    rows, width = images.shape
    own = captions.shape[0]
    pair, half = 2 * own, own // 2
    ranks = taxon_paths.shape[0]
    slots = 2 * NY * NH
    chips = NY * NH
    vmem = pl.BlockSpec(memory_space=pltpu.VMEM)
    dma = pltpu.SemaphoreType.DMA
    scratch = [
        pltpu.VMEM((slots, own, width), BF16),
        pltpu.VMEM((width, rows), BF16),
        pltpu.VMEM((slots, 8, 128), jnp.int32),
        pltpu.VMEM((chips, pair, rows), F32),
        pltpu.VMEM((chips, pair, rows), F32),
        pltpu.VMEM((NY, pair, rows), BF16),
        pltpu.VMEM((NH, NY, pair, rows), BF16),
        pltpu.VMEM((width, rows), F32),
        pltpu.VMEM((width, rows), F32),
        pltpu.VMEM((8, rows), F32),
        pltpu.VMEM((8, rows), F32),
        pltpu.VMEM((NL * NX, 8, rows), F32),
        pltpu.VMEM((chips, pair, width), F32),
        pltpu.VMEM((chips, own, width), BF16),
        pltpu.VMEM((chips, own, width), BF16),
        pltpu.VMEM((NH, own, width), BF16),
        pltpu.VMEM((NH, own, width), BF16),
        pltpu.VMEM((NH, 2, own, width), BF16),
        pltpu.VMEM((NH, 2, own, width), BF16),
        pltpu.VMEM((own, width), BF16),
        pltpu.VMEM((own, width), BF16),
        pltpu.VMEM((2, own, width), BF16),
        pltpu.VMEM((2, own, width), BF16),
        pltpu.VMEM((NL, NX, own, width), BF16),
        pltpu.VMEM((NX, NL, own, width), BF16),
        pltpu.VMEM((own, width), BF16),
        pltpu.VMEM((own, width), BF16),
        dma((64,)), dma((slots,)), dma((8,)), dma((8,)), dma((8,)), dma((8,)),
        dma((chips,)), dma((chips,)), dma((NH, 2)), dma((NH, 2)), dma((NH, 2)), dma((NH, 2)),
        dma((2,)), dma((2,)), dma((2,)), dma((2,)),
        dma((NX,)), dma((NX,)), dma((1,)), dma((1,)),
    ]
    out = jax.ShapeDtypeStruct((own, width), F32)
    pairs = slots * own * rows
    return pl.pallas_call(
        kernel,
        out_shape=(out, out),
        in_specs=[vmem, vmem, vmem, vmem, pl.BlockSpec(memory_space=pltpu.SMEM)],
        out_specs=(vmem, vmem),
        scratch_shapes=scratch,
        compiler_params=pltpu.CompilerParams(
            collective_id=0, has_side_effects=True, vmem_limit_bytes=58 * 1024 * 1024
        ),
        cost_estimate=pl.CostEstimate(
            flops=8 * pairs * width, bytes_accessed=4 * rows * width, transcendentals=pairs
        ),
    )(images, captions, taxon_paths, sample_weight.reshape(1, rows), depth_weight)


def solution(mesh):
    return jax.shard_map(
        body,
        mesh=mesh,
        in_specs=(P("wide", None), P(("wide", "narrow"), None), P(None, "wide"), P("wide"), P()),
        out_specs=(P(("wide", "narrow"), None), P(("wide", "narrow"), None)),
        check_vma=False,
    )
```

time: 323 us -> 95.8 us (0.30)
  waiting for transfers between devices: 127 us -> 0 us
  Pallas kernels: 0 us -> 91.4 us
  blocking collectives: 77.5 us -> 0 us
  other arithmetic: 53.3 us -> 0 us
  matrix products: 46.4 us -> 0 us
  between operations: 13.8 us -> 0.65 us
    reduce_scatter x2 -> x0, waiting for transfers between devices: 126 us -> none  [the longest x1 117 us: body(): lax.psum_scatter(score_scale * jnp.dot(grad_scores.T, images, preferred_e...]
    pallas_call x0 -> x1, Pallas kernels: none -> 91.4 us  [body(): pl.pallas_call(kernel, out_shape=(out, out), in_specs=[vmem, vmem, vmem,...]
    all_gather x1 -> x0, blocking collectives: 49.4 us -> none  [body(): lax.all_gather(own_paths, 'wide', axis=0, tiled=True)]
    dot_general x3 -> x0, matrix products: 46.4 us -> none  [the longest x1 30.6 us: body(): jnp.dot(grad_scores.T, images, preferred_element_type=jnp.float32)]
    reduce_sum x2 -> x0, other arithmetic: 28.8 us -> none  [the longest x1 21.2 us: body(): jnp.sum(weights, axis=1)]
    convert_element_type x1 -> x0, other arithmetic: 22.2 us -> none  [body(): weights.astype(jnp.bfloat16)]
    pmax x1 -> x0, blocking collectives: 15.1 us -> none  [body(): global_peak = lax.pmax(row_peak, 'narrow')]
    psum x1 -> x0, blocking collectives: 12.9 us -> none  [body(): lax.psum((exp_total * jnp.exp(row_peak - global_peak), weight_total), 'na...]
  transfers between devices with their start and end apart: 3 -> 0, of which waited for: 2 -> 0; matrix products, arithmetic and copies ran while one was open for 24% -> 0% of each run, Pallas kernels for 0% -> 0%
where the time goes in v1:
time: 95.8 us; the launch traced here: 95.7 us
  Pallas kernels  91.4 us (95%)
  local copies, waits for them, and re-layouts  3.6 us (4%)
    pallas_call x1, Pallas kernels, body(): pl.pallas_call(kernel, out_shape=(out, out), in_specs=[vmem, vmem, vmem,...  91.4 us
    unnamed x4, local copies, waits for them, and re-layouts  2.34 us

profile of v1, /device:TPU:1, one launch (start us, length us, event | category | flops | bytes accessed | tf_op | source)
XLA Modules:
  0.0 95.7 jit_solution(3483029345923054361)
XLA Ops:
  0.6 1.3 %reshape.7.sw_ref = f32[1,768]{1,0:T(1,128)} reshape(f32[768]{0:T(1024)} %param.8) | data formatting | bytes 6144 | tf_op jit(solution)/shard_map/reshape | solution.py:392
  1.9 91.4 %shard_map.68 = (f32[96,512]{1,0:T(8,128)}, f32[96,512]{1,0:T(8,128)}) custom-call(bf16[768,512]{1,0:T(8,128)(2,1)} %img_ref.1, bf16[96,512]{1,0:T(8,128)(2,1)} %cap_ref.1, s32[7,768]{1,0:T(8,128)} %tax_ref.1, f32[1,768]{1,0:T(1,128)} %reshape.7.sw_ref, f32[8]{0:T(128)} %dw_ref.1), custom_call_target="tpu_custom_call" | custom-call | flops 9663676416 | bytes 1572864 | tf_op jit(solution)/shard_map/pallas_call | solution.py:380
  93.3 0.0 copy-start
  93.3 1.7 %copy.9 = f32[96,512]{1,0:T(8,128)} copy(f32[96,512]{1,0:T(8,128)} %get-tuple-element.4) | data formatting | bytes 393216
  95.0 0.0 copy-done
  95.0 0.7 copy.10
Async XLA Ops:
  93.3 1.7 %copy-start = (f32[96,512]{1,0:T(8,128)S(1)}, f32[96,512]{1,0:T(8,128)}, u32[]{:S(2)}) copy-start(f32[96,512]{1,0:T(8,128)} %get-tuple-element.5) | copy-start | bytes 589828

commit v2 on v1

v2 whole, which is shorter than its diff:
```python
import functools
import math

import jax
import jax.numpy as jnp
from jax import lax
from jax.experimental import pallas as pl
from jax.experimental.pallas import tpu as pltpu
from jax.sharding import PartitionSpec as P

BF16, F32 = jnp.bfloat16, jnp.float32
NY, NH, NX, NL = 4, 4, 4, 2
LANES = 128


def id_codes(ids):
    return ((ids & 127) + 128).astype(F32) * jnp.exp2((ids >> 7).astype(F32))


def kernel(
    img_ref, cap_ref, tax_ref, sw_ref, dw_ref, gi_ref, gc_ref,
    caps, img_t, ids, row_codes, col_codes, e_buf, e_low, t_high, t_low, acc_e, acc_t, t_sum, peaks,
    stat_out, stat_in,
    p_own, p_out, p_in, ya_out, ya_in, zs_out, zs_in, yf_out, yf_in, zf_out, zf_in,
    x_out, x_in, l_out, l_in,
    cap_send, cap_recv, id_send, id_recv, stat_send, stat_recv,
    p_send, p_recv, ya_send, ya_recv, zs_send, zs_recv, yf_send, yf_recv, zf_send, zf_recv,
    x_send, x_recv, l_send, l_recv,
):
    rows, width = img_ref.shape
    own = cap_ref.shape[0]
    pair = 2 * own
    ranks = tax_ref.shape[0]
    scale = width ** -0.5
    to_exp2 = scale * math.log2(math.e)

    wide, narrow = lax.axis_index("wide"), lax.axis_index("narrow")
    core, h, y = wide % 2, (wide // 2) % NH, wide // (2 * NH)
    x, low = narrow % NX, narrow // NX
    near, back = 1 + 2 * core, 3 - 2 * core

    def chip(dy, dh):
        return ((y + dy) % NY) * NH + (h + dh) % NH

    def slot(dy, dh, dc=0):
        return chip(dy, dh) * 2 + (core + dc) % 2

    def at_wide(dy, dh, dc=0):
        return {"wide": slot(dy, dh, dc)}

    def at_narrow(dx, dl):
        return {"narrow": ((low + dl) % NL) * NX + (x + dx) % NX}

    barrier = pltpu.get_barrier_semaphore()
    partners = [at_wide(0, 0, 1)]
    partners += [at_wide(0, d) for d in range(1, NH)] + [at_wide(d, 0) for d in range(1, NY)]
    partners += [at_narrow(dx, dl) for dl in range(NL) for dx in range(NX) if dx or dl]
    for partner in partners:
        pl.semaphore_signal(barrier, inc=1, device_id=partner, device_id_type=pl.DeviceIdType.MESH)

    sent = []

    def send(src, dst, send_sem, recv_sem, where):
        copy = pltpu.make_async_remote_copy(
            src_ref=src, dst_ref=dst, send_sem=send_sem, recv_sem=recv_sem,
            device_id=where, device_id_type=pl.DeviceIdType.MESH,
        )
        copy.start()
        sent.append(copy)

    def arrived(dst, recv_sem):
        pltpu.make_async_copy(dst, dst, recv_sem).wait()

    caps[pl.ds(wide, 1)] = cap_ref[...][None]
    own_rows = tax_ref[...]
    all_ids = jnp.concatenate([own_rows, jnp.zeros((8 - ranks, rows), jnp.int32)], axis=0)
    ids[pl.ds(wide, 1)] = pltpu.roll(all_ids, (rows - own * narrow) % rows, 1)[:, :LANES][None]
    codes = id_codes(own_rows)
    for k in range(ranks):
        row_codes[k] = jnp.broadcast_to(codes[k : k + 1], (16, rows)).astype(BF16)
    img_t[...] = img_ref[...].T
    t_sum[...] = jnp.zeros_like(t_sum)

    pl.semaphore_wait(barrier, len(partners))

    cap_sends = iter(range(64))

    def send_caps(s, where):
        send(caps.at[s], caps.at[s], cap_send.at[next(cap_sends)], cap_recv.at[s], where)

    def caps_arrived(s):
        arrived(caps.at[s], cap_recv.at[s])

    mine = ids.at[pl.ds(wide, 1)]
    send(mine, mine, id_send.at[0], id_recv.at[0], at_wide(0, 0, 1))
    send_caps(wide, at_wide(0, near))
    send_caps(wide, at_wide(1, 0))
    send_caps(wide, at_wide(3, 0))
    send_caps(wide, at_wide(2, 0))
    send_caps(wide, at_wide(0, 2))
    send_caps(wide, at_wide(0, back))
    send_caps(wide, at_wide(0, 0, 1))

    def on_y(s):
        for dy in (1, 3, 2):
            send_caps(s, at_wide(dy, 0))

    def to_core(s):
        send_caps(s, at_wide(0, 0, 1))

    def targets(dy):
        base = 2 * NH * ((y + dy) % NY)
        turned = [id_codes(ids[base + i]).T[:own] for i in range(2 * NH)]
        select = lax.broadcasted_iota(jnp.int32, (8, ranks * LANES), 1) // LANES
        select = (select == lax.broadcasted_iota(jnp.int32, (8, ranks * LANES), 0)).astype(BF16)
        col_codes[...] = jnp.dot(
            jnp.concatenate(turned, axis=0).astype(BF16), select, preferred_element_type=F32
        ).astype(BF16)
        values = [jnp.full((16, 256), dw_ref[k], F32) for k in range(ranks + 1)]
        highs = [v.astype(BF16) for v in values]
        lows = [(v - w.astype(F32)).astype(BF16) for v, w in zip(values, highs)]
        size = 32

        def step(i, carry):
            for r in range(0, own, size):
                for c in range(0, rows, 256):
                    cut = slice(c, c + 256)
                    high = jnp.broadcast_to(highs[0][None], (size // 16, 16, 256))
                    rest = jnp.broadcast_to(lows[0][None], (size // 16, 16, 256))
                    for k in range(ranks):
                        col = col_codes[pl.ds(i * own + r, size), k * LANES : (k + 1) * LANES]
                        col = col.reshape(size // 16, 16, LANES)
                        same = jnp.concatenate([col, col], axis=2) == row_codes[k, :, cut][None]
                        high = jnp.where(same, highs[k + 1][None], high)
                        rest = jnp.where(same, lows[k + 1][None], rest)
                    t_high[base + i, pl.ds(r, size), cut] = high.reshape(size, 256)
                    t_low[base + i, pl.ds(r, size), cut] = rest.reshape(size, 256)
                    t_sum[:, cut] += jnp.sum(high.astype(F32) + rest.astype(F32), axis=0)
            return carry

        lax.fori_loop(0, 2 * NH, step, 0, unroll=4)

    def products(slots, biggest):
        for first, second in zip(slots[::2], slots[1::2]):
            block = jnp.concatenate([caps[first], caps[second]], axis=0)
            s = jnp.dot(block, img_t[...], preferred_element_type=F32)
            e_buf[first] = s[:own]
            e_buf[second] = s[own:]
            biggest = jnp.maximum(biggest, jnp.max(s.reshape(pair // 8, 8, rows), axis=0))
        return biggest

    def exponentials(slots, order, peak, biggest, total):
        new_peak = jnp.max(biggest, axis=0, keepdims=True)
        shrink = jnp.exp2((peak - new_peak) * to_exp2)
        part = jnp.zeros((8, rows), F32)
        for s in slots:
            e = jnp.exp2((e_buf[s] - new_peak) * to_exp2)
            e_buf[s] = e
            e_low[s] = e.astype(BF16)
            part = part + jnp.sum(e.reshape(own // 8, 8, rows), axis=0)
        peaks[order : order + 1] = new_peak
        return new_peak, shrink, total * shrink + jnp.sum(part, axis=0, keepdims=True)

    def moments(slots, shrink, first):
        turned = jnp.concatenate([caps[s] for s in slots], axis=0).T
        for j in range(0, rows, 256):
            cut = slice(j, j + 256)
            low_e = jnp.concatenate([e_low[s, :, cut] for s in slots], axis=0)
            high_t = jnp.concatenate([t_high[s, :, cut] for s in slots], axis=0)
            new_e = jnp.dot(turned, low_e, preferred_element_type=F32)
            new_t = jnp.dot(turned, high_t, preferred_element_type=F32)
            if first:
                acc_e[:, cut] = new_e
                acc_t[:, cut] = new_t
            else:
                acc_e[:, cut] = acc_e[:, cut] * shrink[:, cut] + new_e
                acc_t[:, cut] = acc_t[:, cut] + new_t

    arrived(ids.at[pl.ds(slot(0, 0, 1), 1)], id_recv.at[0])
    both = ids.at[pl.ds(2 * chip(0, 0), 2)]
    for d in range(1, NH):
        send(both, both, id_send.at[d], id_recv.at[NH - d], at_wide(0, d))

    caps_arrived(slot(0, back))
    on_y(slot(0, back))
    to_core(slot(0, back))
    for d in range(1, NH):
        arrived(ids.at[pl.ds(2 * chip(0, d), 2)], id_recv.at[d])
    column = ids.at[pl.ds(2 * NH * y, 2 * NH)]
    for d in range(1, NY):
        send(column, column, id_send.at[NH - 1 + d], id_recv.at[NH - 1 + NY - d], at_wide(d, 0))
    for dy in (1, 3, 2):
        caps_arrived(slot(dy, 0))
        send_caps(slot(dy, 0), at_wide(0, back))
        to_core(slot(dy, 0))
    targets(0)
    first = [slot(dy, 0, dc) for dy in range(NY) for dc in (0, 1)]
    for dy in range(NY):
        caps_arrived(slot(dy, 0, 1))
    peak = jnp.full((1, rows), -jnp.inf, F32)
    exp_total = jnp.zeros((1, rows), F32)
    biggest = products(first, jnp.broadcast_to(peak, (8, rows)))
    caps_arrived(slot(0, 2))
    on_y(slot(0, 2))
    to_core(slot(0, 2))
    peak, shrink, exp_total = exponentials(first, 0, peak, biggest, exp_total)
    caps_arrived(slot(0, near))
    to_core(slot(0, near))
    for dy in range(1, NY):
        arrived(ids.at[pl.ds(2 * NH * ((y + dy) % NY), 2 * NH)], id_recv.at[NH - 1 + dy])
        targets(dy)
    moments(first, shrink, True)
    for dy in (1, 3, 2):
        caps_arrived(slot(dy, back))
        to_core(slot(dy, back))
    for dh in (2, near, back):
        caps_arrived(slot(0, dh, 1))
    for dy in (1, 3, 2):
        caps_arrived(slot(dy, near, 1))
    second = [slot(0, dh, dc) for dh in (2, near, back) for dc in (0, 1)]
    for dy in (1, 3, 2):
        second += [slot(dy, back), slot(dy, near, 1)]
    biggest = products(second, jnp.broadcast_to(peak, (8, rows)))
    peak, shrink, exp_total = exponentials(second, 1, peak, biggest, exp_total)
    moments(second, shrink, False)
    for dy in (1, 3, 2):
        for dh in (2, near):
            caps_arrived(slot(dy, dh))
            to_core(slot(dy, dh))
    third = []
    biggest = jnp.broadcast_to(peak, (8, rows))
    for dy in (1, 3, 2):
        caps_arrived(slot(dy, 2, 1))
        caps_arrived(slot(dy, back, 1))
        more = [slot(dy, 2), slot(dy, 2, 1), slot(dy, near), slot(dy, back, 1)]
        biggest = products(more, biggest)
        third += more
    peak, shrink, exp_total = exponentials(third, 2, peak, biggest, exp_total)

    stat_out[...] = jnp.concatenate(
        [peak, exp_total, jnp.sum(t_sum[...], axis=0, keepdims=True), jnp.zeros((5, rows), F32)], axis=0
    )
    k = 0
    for dl in range(NL):
        for dx in range(NX):
            if dx or dl:
                theirs = ((NL - dl) % NL) * NX + (NX - dx) % NX
                send(stat_out, stat_in.at[theirs], stat_send.at[k], stat_recv.at[theirs], at_narrow(dx, dl))
                k += 1
    moments(third, shrink, False)
    for k in range(1, NL * NX):
        arrived(stat_in.at[k], stat_recv.at[k])
    stats = [stat_out[...]] + [stat_in[k] for k in range(1, NL * NX)]
    top = functools.reduce(jnp.maximum, [s[0:1] for s in stats])
    exp_all = sum(s[1:2] * jnp.exp2((s[0:1] - top) * to_exp2) for s in stats)
    t_all = sum(s[2:3] for s in stats)
    factor_e = sw_ref[...].reshape(1, rows) / exp_all
    factor_t = sw_ref[...].reshape(1, rows) / t_all
    to_e = [factor_e * jnp.exp2((peaks[i : i + 1] - top) * to_exp2) for i in range(3)]

    def group(dy, dh, c):
        if dh == 0:
            return 0
        if dy == 0:
            return 1
        if dh == 2:
            return 2
        return 1 if dh == 3 - 2 * c else 2

    def terms(dy, dh):
        g, k = chip(dy, dh), dy * NH + dh
        grads = []
        for c in (0, 1):
            s = 2 * g + c
            target = t_high[s].astype(F32) + t_low[s].astype(F32)
            grads.append((to_e[group(dy, dh, c)] * e_buf[s] - factor_t * target).astype(BF16))
        p_own[k] = scale * jnp.dot(jnp.concatenate(grads, axis=0), img_ref[...], preferred_element_type=F32)
        p_out[k] = p_own[k, pl.ds((1 - core) * own, own), :].astype(BF16)
        send(p_out.at[k], p_in.at[k], p_send.at[k], p_recv.at[k], at_wide(0, 0, 1))

    def chip_sum(dy, dh):
        k = dy * NH + dh
        arrived(p_in.at[k], p_recv.at[k])
        return p_own[k, pl.ds(core * own, own), :] + p_in[k].astype(F32)

    def over_y(dy, which):
        ya_out[which, dy] = chip_sum(dy, (2, near)[which]).astype(BF16)
        send(
            ya_out.at[which, dy], ya_in.at[which, NY - dy], ya_send.at[which, dy], ya_recv.at[which, NY - dy],
            at_wide(dy, 0),
        )

    def over_z(dy):
        zs_out[dy] = chip_sum(dy, back).astype(BF16)
        send(zs_out.at[dy], zs_in.at[dy], zs_send.at[dy], zs_recv.at[dy], at_wide(0, back))

    def last_y(dy):
        arrived(zs_in.at[dy], zs_recv.at[dy])
        yf_out[dy] = (chip_sum(dy, 0) + zs_in[dy].astype(F32)).astype(BF16)
        send(yf_out.at[dy], yf_in.at[NY - dy], yf_send.at[dy], yf_recv.at[NY - dy], at_wide(dy, 0))

    def last_z(which):
        dh = (2, near, back)[which]
        value = chip_sum(0, dh)
        if which < 2:
            for dy in range(1, NY):
                arrived(ya_in.at[which, dy], ya_recv.at[which, dy])
                value = value + ya_in[which, dy].astype(F32)
        zf_out[which] = value.astype(BF16)
        send(zf_out.at[which], zf_in.at[which], zf_send.at[which], zf_recv.at[which], at_wide(0, dh))

    def last():
        value = chip_sum(0, 0)
        for dy in range(1, NY):
            arrived(yf_in.at[dy], yf_recv.at[dy])
            value = value + yf_in[dy].astype(F32)
        for which in range(3):
            arrived(zf_in.at[which], zf_recv.at[which])
            value = value + zf_in[which].astype(F32)
        gc_ref[...] = value

    def image_terms():
        own_e = scale * factor_e * jnp.exp2((peak - top) * to_exp2)
        own_t = scale * factor_t
        turned = (acc_e[...] * own_e - acc_t[...] * own_t).T
        x_out[...] = turned.reshape(NL, NX, own, width).astype(BF16)
        for d in range(1, NX):
            to = (x + d) % NX
            send(x_out.at[:, to], x_in.at[NX - d], x_send.at[d], x_recv.at[NX - d], at_narrow(d, 0))

    def image_sum():
        for d in range(1, NX):
            arrived(x_in.at[d], x_recv.at[d])

        def total(which):
            value = x_out[which, x].astype(F32)
            for d in range(1, NX):
                value = value + x_in[d, which].astype(F32)
            return value

        l_out[...] = total(1 - low).astype(BF16)
        send(l_out, l_in, l_send.at[0], l_recv.at[0], at_narrow(0, 1))
        gi_ref[...] = total(low)

    def image_finish():
        arrived(l_in, l_recv.at[0])
        gi_ref[...] = gi_ref[...] + l_in[...].astype(F32)

    for step in ((1, 2), (3, 2), (2, 2), (1, 1), (1, 3)):
        terms(*step)
    over_y(1, 0)
    terms(3, 1)
    terms(3, 3)
    over_y(3, 0)
    over_y(2, 0)
    terms(2, 1)
    terms(2, 3)
    over_z(1)
    over_y(1, 1)
    image_terms()
    over_z(3)
    over_y(3, 1)
    over_z(2)
    over_y(2, 1)
    terms(0, 1)
    terms(0, 3)
    terms(0, 2)
    terms(1, 0)
    last_z(2)
    terms(3, 0)
    terms(2, 0)
    terms(0, 0)
    last_z(0)
    for dy in (1, 3, 2):
        last_y(dy)
    last_z(1)
    image_sum()
    image_finish()
    last()
    for copy in sent:
        copy.wait_send()


def body(images, captions, taxon_paths, sample_weight, depth_weight):
    rows, width = images.shape
    own = captions.shape[0]
    pair = 2 * own
    ranks = taxon_paths.shape[0]
    slots = 2 * NY * NH
    chips = NY * NH
    vmem = pl.BlockSpec(memory_space=pltpu.VMEM)
    dma = pltpu.SemaphoreType.DMA
    scratch = [
        pltpu.VMEM((slots, own, width), BF16),
        pltpu.VMEM((width, rows), BF16),
        pltpu.VMEM((slots, 8, LANES), jnp.int32),
        pltpu.VMEM((ranks, 16, rows), BF16),
        pltpu.VMEM((2 * NH * own, ranks * LANES), BF16),
        pltpu.VMEM((slots, own, rows), F32),
        pltpu.VMEM((slots, own, rows), BF16),
        pltpu.VMEM((slots, own, rows), BF16),
        pltpu.VMEM((slots, own, rows), BF16),
        pltpu.VMEM((width, rows), F32),
        pltpu.VMEM((width, rows), F32),
        pltpu.VMEM((16, rows), F32),
        pltpu.VMEM((8, rows), F32),
        pltpu.VMEM((8, rows), F32),
        pltpu.VMEM((NL * NX, 8, rows), F32),
        pltpu.VMEM((chips, pair, width), F32),
        pltpu.VMEM((chips, own, width), BF16),
        pltpu.VMEM((chips, own, width), BF16),
        pltpu.VMEM((2, NY, own, width), BF16),
        pltpu.VMEM((2, NY, own, width), BF16),
        pltpu.VMEM((NY, own, width), BF16),
        pltpu.VMEM((NY, own, width), BF16),
        pltpu.VMEM((NY, own, width), BF16),
        pltpu.VMEM((NY, own, width), BF16),
        pltpu.VMEM((3, own, width), BF16),
        pltpu.VMEM((3, own, width), BF16),
        pltpu.VMEM((NL, NX, own, width), BF16),
        pltpu.VMEM((NX, NL, own, width), BF16),
        pltpu.VMEM((own, width), BF16),
        pltpu.VMEM((own, width), BF16),
        dma((64,)), dma((slots,)), dma((8,)), dma((8,)), dma((8,)), dma((8,)),
        dma((chips,)), dma((chips,)), dma((2, NY)), dma((2, NY)), dma((NY,)), dma((NY,)),
        dma((NY,)), dma((NY,)), dma((3,)), dma((3,)),
        dma((NX,)), dma((NX,)), dma((1,)), dma((1,)),
    ]
    out = jax.ShapeDtypeStruct((own, width), F32)
    pairs = slots * own * rows
    return pl.pallas_call(
        kernel,
        out_shape=(out, out),
        in_specs=[vmem, vmem, vmem, vmem, pl.BlockSpec(memory_space=pltpu.SMEM)],
        out_specs=(vmem, vmem),
        scratch_shapes=scratch,
        compiler_params=pltpu.CompilerParams(
            collective_id=0, has_side_effects=True, vmem_limit_bytes=58 * 1024 * 1024
        ),
        cost_estimate=pl.CostEstimate(
            flops=8 * pairs * width, bytes_accessed=4 * rows * width, transcendentals=pairs
        ),
    )(images, captions, taxon_paths, sample_weight, depth_weight)


def solution(mesh):
    return jax.shard_map(
        body,
        mesh=mesh,
        in_specs=(P("wide", None), P(("wide", "narrow"), None), P(None, "wide"), P("wide"), P()),
        out_specs=(P(("wide", "narrow"), None), P(("wide", "narrow"), None)),
        check_vma=False,
    )
```

time: 95.8 us -> 75.4 us (0.79)
  Pallas kernels: 91.4 us -> 72.3 us
  local copies, waits for them, and re-layouts: 3.6 us -> 2.34 us
    pallas_call x1, Pallas kernels: 91.4 us -> 72.3 us  [body(): pl.pallas_call(kernel, out_shape=(out, out), in_specs=[vmem, vmem, vmem,...]
    reshape x1 -> x0, local copies, waits for them, and re-layouts: 1.27 us -> none  [body(): sample_weight.reshape(1, rows)]
where the time goes in v2:
time: 75.4 us; the launch traced here: 75.3 us
  Pallas kernels  72.3 us (96%)
  local copies, waits for them, and re-layouts  2.34 us (3%)
    pallas_call x1, Pallas kernels, body(): pl.pallas_call(kernel, out_shape=(out, out), in_specs=[vmem, vmem, vmem,...  72.3 us
    unnamed x4, local copies, waits for them, and re-layouts  2.34 us

profile of v2, /device:TPU:1, one launch (start us, length us, event | category | flops | bytes accessed | tf_op | source)
XLA Modules:
  0.0 75.3 jit_solution(3919480799790854348)
XLA Ops:
  0.6 72.3 %shard_map.68 = (f32[96,512]{1,0:T(8,128)}, f32[96,512]{1,0:T(8,128)}) custom-call(bf16[768,512]{1,0:T(8,128)(2,1)} %img_ref.1, bf16[96,512]{1,0:T(8,128)(2,1)} %cap_ref.1, s32[7,768]{1,0:T(8,128)} %tax_ref.1, f32[768]{0:T(1024)} %sw_ref.1, f32[8]{0:T(128)} %dw_ref.1), custom_call_target="tpu_custom_call" | custom-call | flops 9663676416 | bytes 1572864 | tf_op jit(solution)/shard_map/pallas_call | solution.py:431
  72.9 0.0 copy-start
  72.9 1.7 %copy.9 = f32[96,512]{1,0:T(8,128)} copy(f32[96,512]{1,0:T(8,128)} %get-tuple-element.4) | data formatting | bytes 393216
  74.6 0.0 copy-done
  74.6 0.7 copy.10
Async XLA Ops:
  72.9 1.7 %copy-start = (f32[96,512]{1,0:T(8,128)S(1)}, f32[96,512]{1,0:T(8,128)}, u32[]{:S(2)}) copy-start(f32[96,512]{1,0:T(8,128)} %get-tuple-element.5) | copy-start | bytes 589828

commit v3 on v2

--- a/solution.py
+++ b/solution.py
@@ -18,12 +18,12 @@
 
 
 def kernel(
-    img_ref, cap_ref, tax_ref, sw_ref, dw_ref, gi_ref, gc_ref,
-    caps, img_t, ids, row_codes, col_codes, e_buf, e_low, t_high, t_low, acc_e, acc_t, t_sum, peaks,
-    stat_out, stat_in,
+    img_hbm, cap_ref, tax_ref, sw_ref, dw_ref, o_ref,
+    img_ref, caps, img_t, codes, row_codes, col_codes, e_buf, e_low, t_high, t_low, acc_e, acc_t, t_sum, peaks,
+    sum_out, sum_in, stat_out, stat_in,
     p_own, p_out, p_in, ya_out, ya_in, zs_out, zs_in, yf_out, yf_in, zf_out, zf_in,
     x_out, x_in, l_out, l_in,
-    cap_send, cap_recv, id_send, id_recv, stat_send, stat_recv,
+    img_sem, cap_send, cap_recv, id_send, id_recv, sum_send, sum_recv, stat_send, stat_recv,
     p_send, p_recv, ya_send, ya_recv, zs_send, zs_recv, yf_send, yf_recv, zf_send, zf_recv,
     x_send, x_recv, l_send, l_recv,
 ):
@@ -51,6 +51,9 @@
     def at_narrow(dx, dl):
         return {"narrow": ((low + dl) % NL) * NX + (x + dx) % NX}
 
+    img_copy = pltpu.make_async_copy(img_hbm, img_ref, img_sem.at[0])
+    img_copy.start()
+
     barrier = pltpu.get_barrier_semaphore()
     partners = [at_wide(0, 0, 1)]
     partners += [at_wide(0, d) for d in range(1, NH)] + [at_wide(d, 0) for d in range(1, NY)]
@@ -71,48 +74,54 @@
     def arrived(dst, recv_sem):
         pltpu.make_async_copy(dst, dst, recv_sem).wait()
 
-    caps[pl.ds(wide, 1)] = cap_ref[...][None]
-    own_rows = tax_ref[...]
-    all_ids = jnp.concatenate([own_rows, jnp.zeros((8 - ranks, rows), jnp.int32)], axis=0)
-    ids[pl.ds(wide, 1)] = pltpu.roll(all_ids, (rows - own * narrow) % rows, 1)[:, :LANES][None]
-    codes = id_codes(own_rows)
-    for k in range(ranks):
-        row_codes[k] = jnp.broadcast_to(codes[k : k + 1], (16, rows)).astype(BF16)
-    img_t[...] = img_ref[...].T
-    t_sum[...] = jnp.zeros_like(t_sum)
-
     pl.semaphore_wait(barrier, len(partners))
 
     cap_sends = iter(range(64))
 
-    def send_caps(s, where):
-        send(caps.at[s], caps.at[s], cap_send.at[next(cap_sends)], cap_recv.at[s], where)
+    def send_caps(s, where, src=None):
+        src = caps.at[s] if src is None else src
+        send(src, caps.at[s], cap_send.at[next(cap_sends)], cap_recv.at[s], where)
 
     def caps_arrived(s):
         arrived(caps.at[s], cap_recv.at[s])
 
-    mine = ids.at[pl.ds(wide, 1)]
-    send(mine, mine, id_send.at[0], id_recv.at[0], at_wide(0, 0, 1))
-    send_caps(wide, at_wide(0, near))
-    send_caps(wide, at_wide(1, 0))
-    send_caps(wide, at_wide(3, 0))
-    send_caps(wide, at_wide(2, 0))
-    send_caps(wide, at_wide(0, 2))
-    send_caps(wide, at_wide(0, back))
-    send_caps(wide, at_wide(0, 0, 1))
-
-    def on_y(s):
-        for dy in (1, 3, 2):
+    for where in ((1, 0), (3, 0), (2, 0)):
+        send_caps(wide, at_wide(*where), cap_ref)
+
+    own_codes = id_codes(tax_ref[...])
+    padded = jnp.concatenate([own_codes, jnp.zeros((8 - ranks, rows), F32)], axis=0)
+    mine = pltpu.roll(padded, (rows - own * narrow) % rows, 1)[:, :LANES]
+    codes[pl.ds(core, 1), pl.ds(chip(0, 0), 1)] = jnp.concatenate([mine, mine], axis=0).astype(BF16)[None, None]
+
+    def code_part(c, first, count):
+        return codes.at[c, pl.ds(first, count)]
+
+    part = code_part(core, chip(0, 0), 1)
+    for d in (1, 3, 2):
+        send(part, part, id_send.at[d], id_recv.at[NH - d], at_wide(0, d))
+    for where in ((0, 1), (0, 3), (0, 2), (0, 0, 1)):
+        send_caps(wide, at_wide(*where), cap_ref)
+
+    caps[pl.ds(wide, 1)] = cap_ref[...][None]
+    for k in range(ranks):
+        row_codes[k] = jnp.broadcast_to(own_codes[k : k + 1], (16, rows)).astype(BF16)
+    t_sum[...] = jnp.zeros_like(t_sum)
+
+    def on_y(s, places):
+        for dy in places:
             send_caps(s, at_wide(dy, 0))
 
     def to_core(s):
         send_caps(s, at_wide(0, 0, 1))
 
     def targets(dy):
-        base = 2 * NH * ((y + dy) % NY)
-        turned = [id_codes(ids[base + i]).T[:own] for i in range(2 * NH)]
-        select = lax.broadcasted_iota(jnp.int32, (8, ranks * LANES), 1) // LANES
-        select = (select == lax.broadcasted_iota(jnp.int32, (8, ranks * LANES), 0)).astype(BF16)
+        first = NH * ((y + dy) % NY)
+        tiles = [[codes[c, first + i].astype(F32)[:8] for c in (0, 1)] for i in range(NH)]
+        turned = [jnp.concatenate(tile, axis=0).T[:own] for tile in tiles]
+        shape = (16, 2 * ranks * LANES)
+        column, row = (lax.broadcasted_iota(jnp.int32, shape, d) for d in (1, 0))
+        block = column // LANES
+        select = (row == block + jnp.where(block >= ranks, 8 - ranks, 0)).astype(BF16)
         col_codes[...] = jnp.dot(
             jnp.concatenate(turned, axis=0).astype(BF16), select, preferred_element_type=F32
         ).astype(BF16)
@@ -122,23 +131,33 @@
         size = 32
 
         def step(i, carry):
-            for r in range(0, own, size):
-                for c in range(0, rows, 256):
-                    cut = slice(c, c + 256)
+            for c, j in ((c, j) for c in (0, 1) for j in range(0, rows, 256)):
+                cut = slice(j, j + 256)
+                small = []
+                for r in range(0, own, size):
                     high = jnp.broadcast_to(highs[0][None], (size // 16, 16, 256))
                     rest = jnp.broadcast_to(lows[0][None], (size // 16, 16, 256))
                     for k in range(ranks):
-                        col = col_codes[pl.ds(i * own + r, size), k * LANES : (k + 1) * LANES]
+                        lane = (c * ranks + k) * LANES
+                        col = col_codes[pl.ds(i * own + r, size), lane : lane + LANES]
                         col = col.reshape(size // 16, 16, LANES)
                         same = jnp.concatenate([col, col], axis=2) == row_codes[k, :, cut][None]
                         high = jnp.where(same, highs[k + 1][None], high)
                         rest = jnp.where(same, lows[k + 1][None], rest)
-                    t_high[base + i, pl.ds(r, size), cut] = high.reshape(size, 256)
-                    t_low[base + i, pl.ds(r, size), cut] = rest.reshape(size, 256)
-                    t_sum[:, cut] += jnp.sum(high.astype(F32) + rest.astype(F32), axis=0)
+                    t_high[2 * (first + i) + c, pl.ds(r, size), cut] = high.reshape(size, 256)
+                    t_low[2 * (first + i) + c, pl.ds(r, size), cut] = rest.reshape(size, 256)
+                    small += [rest[q] for q in range(size // 16)]
+                while len(small) > 1:
+                    small = [a + b for a, b in zip(small[::2], small[1::2])] + small[len(small) // 2 * 2 :]
+                t_sum[:, cut] += small[0].astype(F32)
             return carry
 
-        lax.fori_loop(0, 2 * NH, step, 0, unroll=4)
+        lax.fori_loop(0, NH, step, 0, unroll=2)
+        ones = jnp.ones((16, 2 * NH * own), BF16)
+        for j in range(0, rows, 256):
+            cut = slice(j, j + 256)
+            block = t_high[pl.ds(2 * first, 2 * NH), :, cut].reshape(2 * NH * own, 256)
+            t_sum[:1, cut] += jnp.dot(ones, block, preferred_element_type=F32)[:1]
 
     def products(slots, biggest):
         for first, second in zip(slots[::2], slots[1::2]):
@@ -176,96 +195,108 @@
                 acc_e[:, cut] = acc_e[:, cut] * shrink[:, cut] + new_e
                 acc_t[:, cut] = acc_t[:, cut] + new_t
 
-    arrived(ids.at[pl.ds(slot(0, 0, 1), 1)], id_recv.at[0])
-    both = ids.at[pl.ds(2 * chip(0, 0), 2)]
-    for d in range(1, NH):
-        send(both, both, id_send.at[d], id_recv.at[NH - d], at_wide(0, d))
-
-    caps_arrived(slot(0, back))
-    on_y(slot(0, back))
-    to_core(slot(0, back))
-    for d in range(1, NH):
-        arrived(ids.at[pl.ds(2 * chip(0, d), 2)], id_recv.at[d])
-    column = ids.at[pl.ds(2 * NH * y, 2 * NH)]
-    for d in range(1, NY):
-        send(column, column, id_send.at[NH - 1 + d], id_recv.at[NH - 1 + NY - d], at_wide(d, 0))
+    def everyone():
+        for dl in range(NL):
+            for dx in range(NX):
+                if dx or dl:
+                    yield dl * NX + dx, ((NL - dl) % NL) * NX + (NX - dx) % NX, at_narrow(dx, dl)
+
+    def folded(row):
+        pieces = [row[:, j : j + LANES] for j in range(0, rows, LANES)]
+        return jnp.concatenate(pieces + [jnp.zeros((8 - len(pieces), LANES), F32)], axis=0)
+
+    def flat(tile):
+        return jnp.concatenate([tile[i : i + 1] for i in range(rows // LANES)], axis=1)
+
+    img_copy.wait()
+    img_t[...] = img_ref[...].T
+
+    for d in (1, 3, 2):
+        arrived(code_part(core, chip(0, d), 1), id_recv.at[d])
+    part = code_part(core, NH * y, NH)
+    for d in (1, 3, 2):
+        send(part, part, id_send.at[NH - 1 + d], id_recv.at[NH - 1 + NY - d], at_wide(d, 0))
+    send(part, part, id_send.at[7], id_recv.at[7], at_wide(0, 0, 1))
+    for dh in (1, 3):
+        caps_arrived(slot(0, dh))
+        on_y(slot(0, dh), (1, 3))
+        to_core(slot(0, dh))
+    arrived(code_part(1 - core, NH * y, NH), id_recv.at[7])
     for dy in (1, 3, 2):
         caps_arrived(slot(dy, 0))
-        send_caps(slot(dy, 0), at_wide(0, back))
+        if dy == 2:
+            send_caps(slot(dy, 0), at_wide(0, 1))
+            send_caps(slot(dy, 0), at_wide(0, 3))
         to_core(slot(dy, 0))
     targets(0)
+    for dy in (1, 3, 2):
+        part = code_part(core, NH * ((y + dy) % NY), NH)
+        arrived(part, id_recv.at[NH - 1 + dy])
+        send(part, part, id_send.at[7 + dy], id_recv.at[7 + dy], at_wide(0, 0, 1))
+    corners = [(dy, dh) for dh in (1, 3) for dy in (1, 3)]
     first = [slot(dy, 0, dc) for dy in range(NY) for dc in (0, 1)]
+    caps_arrived(slot(0, 2))
+    on_y(slot(0, 2), (2, 1, 3))
+    to_core(slot(0, 2))
     for dy in range(NY):
         caps_arrived(slot(dy, 0, 1))
     peak = jnp.full((1, rows), -jnp.inf, F32)
     exp_total = jnp.zeros((1, rows), F32)
     biggest = products(first, jnp.broadcast_to(peak, (8, rows)))
-    caps_arrived(slot(0, 2))
-    on_y(slot(0, 2))
-    to_core(slot(0, 2))
     peak, shrink, exp_total = exponentials(first, 0, peak, biggest, exp_total)
-    caps_arrived(slot(0, near))
-    to_core(slot(0, near))
-    for dy in range(1, NY):
-        arrived(ids.at[pl.ds(2 * NH * ((y + dy) % NY), 2 * NH)], id_recv.at[NH - 1 + dy])
+    for dy in (1, 3, 2):
+        arrived(code_part(1 - core, NH * ((y + dy) % NY), NH), id_recv.at[7 + dy])
         targets(dy)
-    moments(first, shrink, True)
-    for dy in (1, 3, 2):
-        caps_arrived(slot(dy, back))
-        to_core(slot(dy, back))
-    for dh in (2, near, back):
-        caps_arrived(slot(0, dh, 1))
-    for dy in (1, 3, 2):
-        caps_arrived(slot(dy, near, 1))
-    second = [slot(0, dh, dc) for dh in (2, near, back) for dc in (0, 1)]
-    for dy in (1, 3, 2):
-        second += [slot(dy, back), slot(dy, near, 1)]
+        if dy == 1:
+            for place in corners:
+                caps_arrived(slot(*place))
+                to_core(slot(*place))
+    sum_out[...] = folded(jnp.sum(t_sum[...], axis=0, keepdims=True))
+    for k, mirror, where in everyone():
+        send(sum_out, sum_in.at[mirror], sum_send.at[k], sum_recv.at[mirror], where)
+    places = [(0, 1), (0, 3), (0, 2)] + corners
+    second = [slot(*place, dc) for place in places for dc in (0, 1)]
+    for place in places:
+        caps_arrived(slot(*place, 1))
     biggest = products(second, jnp.broadcast_to(peak, (8, rows)))
     peak, shrink, exp_total = exponentials(second, 1, peak, biggest, exp_total)
-    moments(second, shrink, False)
-    for dy in (1, 3, 2):
-        for dh in (2, near):
-            caps_arrived(slot(dy, dh))
-            to_core(slot(dy, dh))
-    third = []
+    shrinks = [shrink]
+    places = [(2, 1), (2, 3), (2, 2), (1, 2), (3, 2)]
+    for place in places:
+        caps_arrived(slot(*place))
+        to_core(slot(*place))
+    third = [slot(*place, dc) for place in places for dc in (0, 1)]
     biggest = jnp.broadcast_to(peak, (8, rows))
-    for dy in (1, 3, 2):
-        caps_arrived(slot(dy, 2, 1))
-        caps_arrived(slot(dy, back, 1))
-        more = [slot(dy, 2), slot(dy, 2, 1), slot(dy, near), slot(dy, back, 1)]
-        biggest = products(more, biggest)
-        third += more
+    for place in places:
+        caps_arrived(slot(*place, 1))
+        biggest = products([slot(*place), slot(*place, 1)], biggest)
     peak, shrink, exp_total = exponentials(third, 2, peak, biggest, exp_total)
-
-    stat_out[...] = jnp.concatenate(
-        [peak, exp_total, jnp.sum(t_sum[...], axis=0, keepdims=True), jnp.zeros((5, rows), F32)], axis=0
-    )
-    k = 0
-    for dl in range(NL):
-        for dx in range(NX):
-            if dx or dl:
-                theirs = ((NL - dl) % NL) * NX + (NX - dx) % NX
-                send(stat_out, stat_in.at[theirs], stat_send.at[k], stat_recv.at[theirs], at_narrow(dx, dl))
-                k += 1
-    moments(third, shrink, False)
-    for k in range(1, NL * NX):
+    shrinks.append(shrink)
+
+    stat_out[...] = jnp.concatenate([folded(peak), folded(exp_total)], axis=0)
+    for k, mirror, where in everyone():
+        send(stat_out, stat_in.at[mirror], stat_send.at[k], stat_recv.at[mirror], where)
+    moments(first, None, True)
+    moments(second, shrinks[0], False)
+    for k, _, _ in everyone():
+        arrived(sum_in.at[k], sum_recv.at[k])
+    t_all = flat(sum_out[...] + sum(sum_in[k] for k, _, _ in everyone()))
+    weight = sw_ref[...].reshape(1, rows)
+    factor_t = weight / t_all
+    moments(third, shrinks[1], False)
+    for k, _, _ in everyone():
         arrived(stat_in.at[k], stat_recv.at[k])
-    stats = [stat_out[...]] + [stat_in[k] for k in range(1, NL * NX)]
-    top = functools.reduce(jnp.maximum, [s[0:1] for s in stats])
-    exp_all = sum(s[1:2] * jnp.exp2((s[0:1] - top) * to_exp2) for s in stats)
-    t_all = sum(s[2:3] for s in stats)
-    factor_e = sw_ref[...].reshape(1, rows) / exp_all
-    factor_t = sw_ref[...].reshape(1, rows) / t_all
+    stats = [stat_out[...]] + [stat_in[k] for k, _, _ in everyone()]
+    top = functools.reduce(jnp.maximum, [s[:8] for s in stats])
+    exp_all = flat(sum(s[8:] * jnp.exp2((s[:8] - top) * to_exp2) for s in stats))
+    top = flat(top)
+    factor_e = weight / exp_all
     to_e = [factor_e * jnp.exp2((peaks[i : i + 1] - top) * to_exp2) for i in range(3)]
 
-    def group(dy, dh, c):
+    def group(dy, dh):
         if dh == 0:
             return 0
-        if dy == 0:
-            return 1
-        if dh == 2:
-            return 2
-        return 1 if dh == 3 - 2 * c else 2
+        return 2 if dy == 2 or (dh == 2 and dy) else 1
 
     def terms(dy, dh):
         g, k = chip(dy, dh), dy * NH + dh
@@ -273,7 +304,7 @@
         for c in (0, 1):
             s = 2 * g + c
             target = t_high[s].astype(F32) + t_low[s].astype(F32)
-            grads.append((to_e[group(dy, dh, c)] * e_buf[s] - factor_t * target).astype(BF16))
+            grads.append((to_e[group(dy, dh)] * e_buf[s] - factor_t * target).astype(BF16))
         p_own[k] = scale * jnp.dot(jnp.concatenate(grads, axis=0), img_ref[...], preferred_element_type=F32)
         p_out[k] = p_own[k, pl.ds((1 - core) * own, own), :].astype(BF16)
         send(p_out.at[k], p_in.at[k], p_send.at[k], p_recv.at[k], at_wide(0, 0, 1))
@@ -317,7 +348,7 @@
         for which in range(3):
             arrived(zf_in.at[which], zf_recv.at[which])
             value = value + zf_in[which].astype(F32)
-        gc_ref[...] = value
+        o_ref[1] = value
 
     def image_terms():
         own_e = scale * factor_e * jnp.exp2((peak - top) * to_exp2)
@@ -340,11 +371,11 @@
 
         l_out[...] = total(1 - low).astype(BF16)
         send(l_out, l_in, l_send.at[0], l_recv.at[0], at_narrow(0, 1))
-        gi_ref[...] = total(low)
+        o_ref[0] = total(low)
 
     def image_finish():
         arrived(l_in, l_recv.at[0])
-        gi_ref[...] = gi_ref[...] + l_in[...].astype(F32)
+        o_ref[0] = o_ref[0] + l_in[...].astype(F32)
 
     for step in ((1, 2), (3, 2), (2, 2), (1, 1), (1, 3)):
         terms(*step)
@@ -391,11 +422,12 @@
     vmem = pl.BlockSpec(memory_space=pltpu.VMEM)
     dma = pltpu.SemaphoreType.DMA
     scratch = [
+        pltpu.VMEM((rows, width), BF16),
         pltpu.VMEM((slots, own, width), BF16),
         pltpu.VMEM((width, rows), BF16),
-        pltpu.VMEM((slots, 8, LANES), jnp.int32),
+        pltpu.VMEM((2, chips, 16, LANES), BF16),
         pltpu.VMEM((ranks, 16, rows), BF16),
-        pltpu.VMEM((2 * NH * own, ranks * LANES), BF16),
+        pltpu.VMEM((NH * own, 2 * ranks * LANES), BF16),
         pltpu.VMEM((slots, own, rows), F32),
         pltpu.VMEM((slots, own, rows), BF16),
         pltpu.VMEM((slots, own, rows), BF16),
@@ -404,8 +436,10 @@
         pltpu.VMEM((width, rows), F32),
         pltpu.VMEM((16, rows), F32),
         pltpu.VMEM((8, rows), F32),
-        pltpu.VMEM((8, rows), F32),
-        pltpu.VMEM((NL * NX, 8, rows), F32),
+        pltpu.VMEM((8, LANES), F32),
+        pltpu.VMEM((NL * NX, 8, LANES), F32),
+        pltpu.VMEM((16, LANES), F32),
+        pltpu.VMEM((NL * NX, 16, LANES), F32),
         pltpu.VMEM((chips, pair, width), F32),
         pltpu.VMEM((chips, own, width), BF16),
         pltpu.VMEM((chips, own, width), BF16),
@@ -421,18 +455,18 @@
         pltpu.VMEM((NX, NL, own, width), BF16),
         pltpu.VMEM((own, width), BF16),
         pltpu.VMEM((own, width), BF16),
-        dma((64,)), dma((slots,)), dma((8,)), dma((8,)), dma((8,)), dma((8,)),
+        dma((1,)), dma((64,)), dma((slots,)), dma((12,)), dma((12,)), dma((8,)), dma((8,)), dma((8,)), dma((8,)),
         dma((chips,)), dma((chips,)), dma((2, NY)), dma((2, NY)), dma((NY,)), dma((NY,)),
         dma((NY,)), dma((NY,)), dma((3,)), dma((3,)),
         dma((NX,)), dma((NX,)), dma((1,)), dma((1,)),
     ]
-    out = jax.ShapeDtypeStruct((own, width), F32)
+    out = jax.ShapeDtypeStruct((2, own, width), F32)
     pairs = slots * own * rows
-    return pl.pallas_call(
+    o = pl.pallas_call(
         kernel,
-        out_shape=(out, out),
-        in_specs=[vmem, vmem, vmem, vmem, pl.BlockSpec(memory_space=pltpu.SMEM)],
-        out_specs=(vmem, vmem),
+        out_shape=out,
+        in_specs=[pl.BlockSpec(memory_space=pl.ANY), vmem, vmem, vmem, pl.BlockSpec(memory_space=pltpu.SMEM)],
+        out_specs=vmem,
         scratch_shapes=scratch,
         compiler_params=pltpu.CompilerParams(
             collective_id=0, has_side_effects=True, vmem_limit_bytes=58 * 1024 * 1024
@@ -441,6 +475,7 @@
             flops=8 * pairs * width, bytes_accessed=4 * rows * width, transcendentals=pairs
         ),
     )(images, captions, taxon_paths, sample_weight, depth_weight)
+    return o[0], o[1]
 
 
 def solution(mesh):

time: 75.4 us -> 68.8 us (0.912)
  Pallas kernels: 72.3 us -> 66 us
    pallas_call x1, Pallas kernels: 72.3 us -> 66 us  [body(): pl.pallas_call(kernel, out_shape=out, in_specs=[pl.BlockSpec(memory_space...]
    unnamed x4 -> x0, local copies, waits for them, and re-layouts: 2.34 us -> none
    squeeze x0 -> x1, local copies, waits for them, and re-layouts: none -> 1.79 us  [body(): return (o[0], o[1])]
where the time goes in v3:
time: 68.8 us; the launch traced here: 68.4 us
  Pallas kernels  66 us (96%)
  local copies, waits for them, and re-layouts  1.79 us (3%)
    pallas_call x1, Pallas kernels, body(): pl.pallas_call(kernel, out_shape=out, in_specs=[pl.BlockSpec(memory_space...  66 us
    squeeze x1, local copies, waits for them, and re-layouts, body(): return (o[0], o[1])  1.79 us

profile of v3, /device:TPU:1, one launch (start us, length us, event | category | flops | bytes accessed | tf_op | source)
XLA Modules:
  0.0 68.4 jit_solution(14382664831992303861)
XLA Ops:
  0.6 66.0 %shard_map.68 = f32[2,96,512]{2,1,0:T(8,128)} custom-call(bf16[768,512]{1,0:T(8,128)(2,1)} %img_hbm.1, bf16[96,512]{1,0:T(8,128)(2,1)} %cap_ref.1, s32[7,768]{1,0:T(8,128)} %tax_ref.1, f32[768]{0:T(1024)} %sw_ref.1, f32[8]{0:T(128)} %dw_ref.1), custom_call_target="tpu_custom_call" | custom-call | flops 9663676416 | bytes 1572864 | tf_op jit(solution)/shard_map/pallas_call | solution.py:465
  66.6 1.8 %slice_bitcast_fusion = (f32[96,512]{1,0:T(8,128)}, f32[96,512]{1,0:T(8,128)}) fusion(f32[2,96,512]{2,1,0:T(8,128)} %shard_map.68), kind=kLoop, calls=%fused_computation | loop fusion | bytes 786432 | tf_op jit(solution)/shard_map/squeeze | solution.py:478

commit v4 on v3

--- a/solution.py
+++ b/solution.py
@@ -19,7 +19,7 @@
 
 def kernel(
     img_hbm, cap_ref, tax_ref, sw_ref, dw_ref, o_ref,
-    img_ref, caps, img_t, codes, row_codes, col_codes, e_buf, e_low, t_high, t_low, acc_e, acc_t, t_sum, peaks,
+    img_ref, caps, img_t, codes, select, row_codes, col_codes, e_buf, e_low, t_high, t_low, acc_e, acc_t, t_sum, peaks,
     sum_out, sum_in, stat_out, stat_in,
     p_own, p_out, p_in, ya_out, ya_in, zs_out, zs_in, yf_out, yf_in, zf_out, zf_in,
     x_out, x_in, l_out, l_in,
@@ -37,8 +37,6 @@
     wide, narrow = lax.axis_index("wide"), lax.axis_index("narrow")
     core, h, y = wide % 2, (wide // 2) % NH, wide // (2 * NH)
     x, low = narrow % NX, narrow // NX
-    near, back = 1 + 2 * core, 3 - 2 * core
-
     def chip(dy, dh):
         return ((y + dy) % NY) * NH + (h + dh) % NH
 
@@ -114,23 +112,19 @@
     def to_core(s):
         send_caps(s, at_wide(0, 0, 1))
 
-    def targets(dy):
+    def targets(dy, beside=()):
         first = NH * ((y + dy) % NY)
         tiles = [[codes[c, first + i].astype(F32)[:8] for c in (0, 1)] for i in range(NH)]
         turned = [jnp.concatenate(tile, axis=0).T[:own] for tile in tiles]
-        shape = (16, 2 * ranks * LANES)
-        column, row = (lax.broadcasted_iota(jnp.int32, shape, d) for d in (1, 0))
-        block = column // LANES
-        select = (row == block + jnp.where(block >= ranks, 8 - ranks, 0)).astype(BF16)
         col_codes[...] = jnp.dot(
-            jnp.concatenate(turned, axis=0).astype(BF16), select, preferred_element_type=F32
+            jnp.concatenate(turned, axis=0).astype(BF16), select[...], preferred_element_type=F32
         ).astype(BF16)
         values = [jnp.full((16, 256), dw_ref[k], F32) for k in range(ranks + 1)]
         highs = [v.astype(BF16) for v in values]
         lows = [(v - w.astype(F32)).astype(BF16) for v, w in zip(values, highs)]
         size = 32
 
-        def step(i, carry):
+        def step(i):
             for c, j in ((c, j) for c in (0, 1) for j in range(0, rows, 256)):
                 cut = slice(j, j + 256)
                 small = []
@@ -150,9 +144,11 @@
                 while len(small) > 1:
                     small = [a + b for a, b in zip(small[::2], small[1::2])] + small[len(small) // 2 * 2 :]
                 t_sum[:, cut] += small[0].astype(F32)
-            return carry
-
-        lax.fori_loop(0, NH, step, 0, unroll=2)
+
+        for i in range(NH):
+            step(i)
+            if i < len(beside):
+                beside[i]()
         ones = jnp.ones((16, 2 * NH * own), BF16)
         for j in range(0, rows, 256):
             cut = slice(j, j + 256)
@@ -208,6 +204,10 @@
     def flat(tile):
         return jnp.concatenate([tile[i : i + 1] for i in range(rows // LANES)], axis=1)
 
+    shape = (16, 2 * ranks * LANES)
+    column, row = (lax.broadcasted_iota(jnp.int32, shape, d) for d in (1, 0))
+    block = column // LANES
+    select[...] = (row == block + jnp.where(block >= ranks, 8 - ranks, 0)).astype(BF16)
     img_copy.wait()
     img_t[...] = img_ref[...].T
 
@@ -242,32 +242,49 @@
         caps_arrived(slot(dy, 0, 1))
     peak = jnp.full((1, rows), -jnp.inf, F32)
     exp_total = jnp.zeros((1, rows), F32)
-    biggest = products(first, jnp.broadcast_to(peak, (8, rows)))
-    peak, shrink, exp_total = exponentials(first, 0, peak, biggest, exp_total)
-    for dy in (1, 3, 2):
+    largest = [jnp.broadcast_to(peak, (8, rows))]
+
+    def pairs(slots):
+        def product(two):
+            largest[0] = products(two, largest[0])
+
+        return [functools.partial(product, slots[i : i + 2]) for i in range(0, len(slots), 2)]
+
+    def code_arrived(dy):
         arrived(code_part(1 - core, NH * ((y + dy) % NY), NH), id_recv.at[7 + dy])
-        targets(dy)
-        if dy == 1:
-            for place in corners:
-                caps_arrived(slot(*place))
-                to_core(slot(*place))
+
+    code_arrived(1)
+    targets(1, pairs(first))
+    peak, shrink, exp_total = exponentials(first, 0, peak, largest[0], exp_total)
+    for place in corners:
+        caps_arrived(slot(*place))
+        to_core(slot(*place))
+    column = [(0, 1), (0, 3), (0, 2)]
+    second = [slot(*place, dc) for place in column + corners for dc in (0, 1)]
+    for place in column:
+        caps_arrived(slot(*place, 1))
+    largest[0] = jnp.broadcast_to(peak, (8, rows))
+    code_arrived(3)
+    targets(3, pairs(second[:6]))
+    code_arrived(2)
+    late = [(2, 1), (2, 3), (2, 2), (1, 2), (3, 2)]
+    for place in corners:
+        caps_arrived(slot(*place, 1))
+    targets(2, pairs(second[6:]))
+    for place in late[:2]:
+        caps_arrived(slot(*place))
+        to_core(slot(*place))
     sum_out[...] = folded(jnp.sum(t_sum[...], axis=0, keepdims=True))
     for k, mirror, where in everyone():
         send(sum_out, sum_in.at[mirror], sum_send.at[k], sum_recv.at[mirror], where)
-    places = [(0, 1), (0, 3), (0, 2)] + corners
-    second = [slot(*place, dc) for place in places for dc in (0, 1)]
-    for place in places:
-        caps_arrived(slot(*place, 1))
-    biggest = products(second, jnp.broadcast_to(peak, (8, rows)))
-    peak, shrink, exp_total = exponentials(second, 1, peak, biggest, exp_total)
-    shrinks = [shrink]
-    places = [(2, 1), (2, 3), (2, 2), (1, 2), (3, 2)]
-    for place in places:
+    for place in late[2:]:
         caps_arrived(slot(*place))
         to_core(slot(*place))
-    third = [slot(*place, dc) for place in places for dc in (0, 1)]
+    peak, shrink, exp_total = exponentials(second, 1, peak, largest[0], exp_total)
+    shrinks = [shrink]
+    third = [slot(*place, dc) for place in late for dc in (0, 1)]
     biggest = jnp.broadcast_to(peak, (8, rows))
-    for place in places:
+    for place in late:
         caps_arrived(slot(*place, 1))
         biggest = products([slot(*place), slot(*place, 1)], biggest)
     peak, shrink, exp_total = exponentials(third, 2, peak, biggest, exp_total)
@@ -314,40 +331,41 @@
         arrived(p_in.at[k], p_recv.at[k])
         return p_own[k, pl.ds(core * own, own), :] + p_in[k].astype(F32)
 
-    def over_y(dy, which):
-        ya_out[which, dy] = chip_sum(dy, (2, near)[which]).astype(BF16)
+    def over_y(dy, dh):
+        ya_out[dy, dh] = chip_sum(dy, dh).astype(BF16)
         send(
-            ya_out.at[which, dy], ya_in.at[which, NY - dy], ya_send.at[which, dy], ya_recv.at[which, NY - dy],
-            at_wide(dy, 0),
+            ya_out.at[dy, dh], ya_in.at[NY - dy, dh], ya_send.at[dy, dh], ya_recv.at[NY - dy, dh], at_wide(dy, 0)
         )
 
-    def over_z(dy):
-        zs_out[dy] = chip_sum(dy, back).astype(BF16)
-        send(zs_out.at[dy], zs_in.at[dy], zs_send.at[dy], zs_recv.at[dy], at_wide(0, back))
+    def over_z(dh):
+        zs_out[dh] = chip_sum(2, dh).astype(BF16)
+        send(zs_out.at[dh], zs_in.at[NH - dh], zs_send.at[dh], zs_recv.at[NH - dh], at_wide(0, dh))
 
     def last_y(dy):
-        arrived(zs_in.at[dy], zs_recv.at[dy])
-        yf_out[dy] = (chip_sum(dy, 0) + zs_in[dy].astype(F32)).astype(BF16)
+        value = chip_sum(dy, 0)
+        if dy == 2:
+            for dh in (1, 3):
+                arrived(zs_in.at[dh], zs_recv.at[dh])
+                value = value + zs_in[dh].astype(F32)
+        yf_out[dy] = value.astype(BF16)
         send(yf_out.at[dy], yf_in.at[NY - dy], yf_send.at[dy], yf_recv.at[NY - dy], at_wide(dy, 0))
 
-    def last_z(which):
-        dh = (2, near, back)[which]
+    def last_z(dh):
         value = chip_sum(0, dh)
-        if which < 2:
-            for dy in range(1, NY):
-                arrived(ya_in.at[which, dy], ya_recv.at[which, dy])
-                value = value + ya_in[which, dy].astype(F32)
-        zf_out[which] = value.astype(BF16)
-        send(zf_out.at[which], zf_in.at[which], zf_send.at[which], zf_recv.at[which], at_wide(0, dh))
+        for dy in (1, 3, 2) if dh == 2 else (1, 3):
+            arrived(ya_in.at[dy, dh], ya_recv.at[dy, dh])
+            value = value + ya_in[dy, dh].astype(F32)
+        zf_out[dh] = value.astype(BF16)
+        send(zf_out.at[dh], zf_in.at[NH - dh], zf_send.at[dh], zf_recv.at[NH - dh], at_wide(0, dh))
 
     def last():
         value = chip_sum(0, 0)
         for dy in range(1, NY):
             arrived(yf_in.at[dy], yf_recv.at[dy])
             value = value + yf_in[dy].astype(F32)
-        for which in range(3):
-            arrived(zf_in.at[which], zf_recv.at[which])
-            value = value + zf_in[which].astype(F32)
+        for dh in range(1, NH):
+            arrived(zf_in.at[dh], zf_recv.at[dh])
+            value = value + zf_in[dh].astype(F32)
         o_ref[1] = value
 
     def image_terms():
@@ -377,34 +395,31 @@
         arrived(l_in, l_recv.at[0])
         o_ref[0] = o_ref[0] + l_in[...].astype(F32)
 
-    for step in ((1, 2), (3, 2), (2, 2), (1, 1), (1, 3)):
+    for step in ((2, 1), (2, 3), (1, 2), (3, 2), (2, 2)):
         terms(*step)
-    over_y(1, 0)
+    over_z(1)
+    over_z(3)
+    terms(1, 1)
     terms(3, 1)
+    for dy in (1, 3, 2):
+        over_y(dy, 2)
+    terms(1, 3)
     terms(3, 3)
-    over_y(3, 0)
-    over_y(2, 0)
-    terms(2, 1)
-    terms(2, 3)
-    over_z(1)
     over_y(1, 1)
+    over_y(3, 1)
     image_terms()
-    over_z(3)
-    over_y(3, 1)
-    over_z(2)
-    over_y(2, 1)
-    terms(0, 1)
+    over_y(1, 3)
+    over_y(3, 3)
+    for step in ((1, 0), (3, 0), (2, 0), (0, 2), (0, 1)):
+        terms(*step)
+    last_y(1)
+    last_y(3)
     terms(0, 3)
-    terms(0, 2)
-    terms(1, 0)
+    terms(0, 0)
     last_z(2)
-    terms(3, 0)
-    terms(2, 0)
-    terms(0, 0)
-    last_z(0)
-    for dy in (1, 3, 2):
-        last_y(dy)
+    last_y(2)
     last_z(1)
+    last_z(3)
     image_sum()
     image_finish()
     last()
@@ -426,6 +441,7 @@
         pltpu.VMEM((slots, own, width), BF16),
         pltpu.VMEM((width, rows), BF16),
         pltpu.VMEM((2, chips, 16, LANES), BF16),
+        pltpu.VMEM((16, 2 * ranks * LANES), BF16),
         pltpu.VMEM((ranks, 16, rows), BF16),
         pltpu.VMEM((NH * own, 2 * ranks * LANES), BF16),
         pltpu.VMEM((slots, own, rows), F32),
@@ -443,21 +459,21 @@
         pltpu.VMEM((chips, pair, width), F32),
         pltpu.VMEM((chips, own, width), BF16),
         pltpu.VMEM((chips, own, width), BF16),
-        pltpu.VMEM((2, NY, own, width), BF16),
-        pltpu.VMEM((2, NY, own, width), BF16),
+        pltpu.VMEM((NY, NH, own, width), BF16),
+        pltpu.VMEM((NY, NH, own, width), BF16),
+        pltpu.VMEM((NH, own, width), BF16),
+        pltpu.VMEM((NH, own, width), BF16),
         pltpu.VMEM((NY, own, width), BF16),
         pltpu.VMEM((NY, own, width), BF16),
-        pltpu.VMEM((NY, own, width), BF16),
-        pltpu.VMEM((NY, own, width), BF16),
-        pltpu.VMEM((3, own, width), BF16),
-        pltpu.VMEM((3, own, width), BF16),
+        pltpu.VMEM((NH, own, width), BF16),
+        pltpu.VMEM((NH, own, width), BF16),
         pltpu.VMEM((NL, NX, own, width), BF16),
         pltpu.VMEM((NX, NL, own, width), BF16),
         pltpu.VMEM((own, width), BF16),
         pltpu.VMEM((own, width), BF16),
         dma((1,)), dma((64,)), dma((slots,)), dma((12,)), dma((12,)), dma((8,)), dma((8,)), dma((8,)), dma((8,)),
-        dma((chips,)), dma((chips,)), dma((2, NY)), dma((2, NY)), dma((NY,)), dma((NY,)),
-        dma((NY,)), dma((NY,)), dma((3,)), dma((3,)),
+        dma((chips,)), dma((chips,)), dma((NY, NH)), dma((NY, NH)), dma((NH,)), dma((NH,)),
+        dma((NY,)), dma((NY,)), dma((NH,)), dma((NH,)),
         dma((NX,)), dma((NX,)), dma((1,)), dma((1,)),
     ]
     out = jax.ShapeDtypeStruct((2, own, width), F32)

time: 68.8 us -> 67.4 us (0.980)
  Pallas kernels: 66 us -> 64.8 us
    pallas_call x1, Pallas kernels: 66 us -> 64.8 us  [body(): pl.pallas_call(kernel, out_shape=out, in_specs=[pl.BlockSpec(memory_space...]
where the time goes in v4:
time: 67.4 us; the launch traced here: 67.3 us
  Pallas kernels  64.8 us (96%)
  local copies, waits for them, and re-layouts  1.79 us (3%)
    pallas_call x1, Pallas kernels, body(): pl.pallas_call(kernel, out_shape=out, in_specs=[pl.BlockSpec(memory_space...  64.8 us
    squeeze x1, local copies, waits for them, and re-layouts, body(): return (o[0], o[1])  1.79 us

profile of v4, /device:TPU:1, one launch (start us, length us, event | category | flops | bytes accessed | tf_op | source)
XLA Modules:
  0.0 67.3 jit_solution(5587657816689482742)
XLA Ops:
  0.6 64.8 %shard_map.68 = f32[2,96,512]{2,1,0:T(8,128)} custom-call(bf16[768,512]{1,0:T(8,128)(2,1)} %img_hbm.1, bf16[96,512]{1,0:T(8,128)(2,1)} %cap_ref.1, s32[7,768]{1,0:T(8,128)} %tax_ref.1, f32[768]{0:T(1024)} %sw_ref.1, f32[8]{0:T(128)} %dw_ref.1), custom_call_target="tpu_custom_call" | custom-call | flops 9663676416 | bytes 1572864 | tf_op jit(solution)/shard_map/pallas_call | solution.py:481
  65.5 1.8 %slice_bitcast_fusion = (f32[96,512]{1,0:T(8,128)}, f32[96,512]{1,0:T(8,128)}) fusion(f32[2,96,512]{2,1,0:T(8,128)} %shard_map.68), kind=kLoop, calls=%fused_computation | loop fusion | bytes 786432 | tf_op jit(solution)/shard_map/squeeze | solution.py:494

commit v5 on v4

--- a/solution.py
+++ b/solution.py
@@ -210,6 +210,10 @@
     select[...] = (row == block + jnp.where(block >= ranks, 8 - ranks, 0)).astype(BF16)
     img_copy.wait()
     img_t[...] = img_ref[...].T
+    peak = jnp.full((1, rows), -jnp.inf, F32)
+    exp_total = jnp.zeros((1, rows), F32)
+    caps_arrived(slot(0, 0, 1))
+    largest = [products([slot(0, 0), slot(0, 0, 1)], jnp.broadcast_to(peak, (8, rows)))]
 
     for d in (1, 3, 2):
         arrived(code_part(core, chip(0, d), 1), id_recv.at[d])
@@ -238,11 +242,8 @@
     caps_arrived(slot(0, 2))
     on_y(slot(0, 2), (2, 1, 3))
     to_core(slot(0, 2))
-    for dy in range(NY):
+    for dy in (1, 2, 3):
         caps_arrived(slot(dy, 0, 1))
-    peak = jnp.full((1, rows), -jnp.inf, F32)
-    exp_total = jnp.zeros((1, rows), F32)
-    largest = [jnp.broadcast_to(peak, (8, rows))]
 
     def pairs(slots):
         def product(two):
@@ -254,7 +255,7 @@
         arrived(code_part(1 - core, NH * ((y + dy) % NY), NH), id_recv.at[7 + dy])
 
     code_arrived(1)
-    targets(1, pairs(first))
+    targets(1, pairs(first[2:]))
     peak, shrink, exp_total = exponentials(first, 0, peak, largest[0], exp_total)
     for place in corners:
         caps_arrived(slot(*place))
@@ -274,9 +275,6 @@
     for place in late[:2]:
         caps_arrived(slot(*place))
         to_core(slot(*place))
-    sum_out[...] = folded(jnp.sum(t_sum[...], axis=0, keepdims=True))
-    for k, mirror, where in everyone():
-        send(sum_out, sum_in.at[mirror], sum_send.at[k], sum_recv.at[mirror], where)
     for place in late[2:]:
         caps_arrived(slot(*place))
         to_core(slot(*place))
@@ -293,6 +291,9 @@
     stat_out[...] = jnp.concatenate([folded(peak), folded(exp_total)], axis=0)
     for k, mirror, where in everyone():
         send(stat_out, stat_in.at[mirror], stat_send.at[k], stat_recv.at[mirror], where)
+    sum_out[...] = folded(jnp.sum(t_sum[...], axis=0, keepdims=True))
+    for k, mirror, where in everyone():
+        send(sum_out, sum_in.at[mirror], sum_send.at[k], sum_recv.at[mirror], where)
     moments(first, None, True)
     moments(second, shrinks[0], False)
     for k, _, _ in everyone():

time: 67.4 us -> 68.3 us (1.013)
  Pallas kernels: 64.8 us -> 65.7 us
    pallas_call x1, Pallas kernels: 64.8 us -> 65.7 us  [body(): pl.pallas_call(kernel, out_shape=out, in_specs=[pl.BlockSpec(memory_space...]
where the time goes in v5:
time: 68.3 us; the launch traced here: 68.2 us
  Pallas kernels  65.7 us (96%)
  local copies, waits for them, and re-layouts  1.79 us (3%)
    pallas_call x1, Pallas kernels, body(): pl.pallas_call(kernel, out_shape=out, in_specs=[pl.BlockSpec(memory_space...  65.7 us
    squeeze x1, local copies, waits for them, and re-layouts, body(): return (o[0], o[1])  1.79 us

profile of v5, /device:TPU:1, one launch (start us, length us, event | category | flops | bytes accessed | tf_op | source)
XLA Modules:
  0.0 68.2 jit_solution(2470415021059044182)
XLA Ops:
  0.6 65.7 %shard_map.68 = f32[2,96,512]{2,1,0:T(8,128)} custom-call(bf16[768,512]{1,0:T(8,128)(2,1)} %img_hbm.1, bf16[96,512]{1,0:T(8,128)(2,1)} %cap_ref.1, s32[7,768]{1,0:T(8,128)} %tax_ref.1, f32[768]{0:T(1024)} %sw_ref.1, f32[8]{0:T(128)} %dw_ref.1), custom_call_target="tpu_custom_call" | custom-call | flops 9663676416 | bytes 1572864 | tf_op jit(solution)/shard_map/pallas_call | solution.py:482
  66.4 1.8 %slice_bitcast_fusion = (f32[96,512]{1,0:T(8,128)}, f32[96,512]{1,0:T(8,128)}) fusion(f32[2,96,512]{2,1,0:T(8,128)} %shard_map.68), kind=kLoop, calls=%fused_computation | loop fusion | bytes 786432 | tf_op jit(solution)/shard_map/squeeze | solution.py:495
